TPU v7x, 512 devices: a whole 4x8x8 slice. The times are simulated.
512 devices in a mesh: src: 16 (over z, core), mod: 32 (over x, y).
Axes of the slice: x: 4, y: 8, z: 8, core: 2. Of those that a mesh axis runs over, the one named last changes fastest.
Arguments:
- right_side: float32 [16, 128, 16, 128], P(None, 'mod'), may hold values from -8 to 8
- depth_weight: float32 [128, 16, 128], P('mod'), may hold values from 0.25 to 2
- panels: bfloat16 [64, 3072, 32, 128], P('src', 'mod'), may hold values from -0.09375 to 0.09375
- data_weight: float32 [64, 3072], P('src', 'mod'), may hold values from 1 to 10
- footprints: int32 [64, 32], replicated, may hold values from 0 to 2047, as said below
- counts: int32 [64], replicated, may hold values from 768 to 3072, as said below
Outputs:
- solution: float32 [16, 128, 16, 128], P(None, 'mod')
- residual: float32 [16, 128, 16, 128], P(None, 'mod')
Inputs may be any that keep to these rules, and one draw needn't show every extreme that they name: `footprints`: each row names 32 distinct tiles; at most 2 of one row's tiles lie among the 64 tiles of one index of mod, and in every row some index of mod holds 2 of them. `counts`: some transmitter has all 3072 rows live.
All inputs are finite; a program needn't handle non-finite values.
Results may differ from a plain program's by a relative error of at most 0.039.
Values may be sent and summed in bfloat16 or wider, within the bound.
No kernel may reach another device: no remote copies, remote signals or barrier semaphores. Data moves between devices by JAX's collectives and lax.ppermute only.
A program may use at most 64 MiB of HBM per device.

v0:
```python
import functools

import jax
import jax.numpy as jnp
from jax import lax
from jax.experimental import pallas as pl
from jax.experimental.pallas import tpu as pltpu
from jax.sharding import PartitionSpec as P

CAP = 2
INNER = 8
NARROW = 48
ITERS = 3
F32 = jnp.float32
BF16 = jnp.bfloat16
VMEM = pl.BlockSpec(memory_space=pltpu.VMEM)
SMEM = pl.BlockSpec(memory_space=pltpu.SMEM)


def call(kernel, outs, args, specs, scratch=(), limit=16 << 20):
    return pl.pallas_call(
        kernel,
        out_shape=[jax.ShapeDtypeStruct(shape, dtype) for shape, dtype in outs],
        in_specs=list(specs),
        out_specs=[VMEM] * len(outs),
        scratch_shapes=list(scratch),
        compiler_params=pltpu.CompilerParams(vmem_limit_bytes=limit),
    )(*args)


def solve_small(system, target):
    size = system.shape[0]
    turned = jnp.concatenate([system, target], axis=0)
    rows = [jnp.broadcast_to(turned[:, i : i + 1], (2 * size, 128)) for i in range(size)]
    for p in range(size):
        base = 8 * ((p + 1) // 8)
        lead = [rows[i][p - (2 * size - rows[i].shape[0])][None, :] for i in range(size)]
        keep = base - (2 * size - rows[0].shape[0])
        pivot = rows[p][keep:] / lead[p]
        rows = [
            pivot if i == p else rows[i][keep:] - lead[i] * pivot for i in range(size)
        ]
    return rows


def matrix_turned(rows):
    lanes = lax.broadcasted_iota(jnp.int32, rows[0].shape, 1)
    total = jnp.zeros(rows[0].shape, F32)
    for i, row in enumerate(rows):
        total = jnp.where(lanes == i, row, total)
    return total[:, : len(rows)]


def split_three(gram):
    size = gram.shape[0]
    high = gram.astype(BF16).astype(F32)
    rest = gram - high
    middle = rest.astype(BF16).astype(F32)
    low = rest - middle
    fill = jnp.zeros((size, 128 - 3 * size), F32)
    return jnp.concatenate([high, middle, low, fill], axis=1).astype(BF16)


def join_three(total):
    size = total.shape[0]
    return total[:, :size] + total[:, size : 2 * size] + total[:, 2 * size : 3 * size]


def read_rows(ref):
    return [ref[i] for i in range(ref.shape[0])]


def mix_tile(tile, spread):
    total = None
    for i, factor in enumerate(spread):
        term = factor * tile[i : i + 1, :]
        total = term if total is None else total + term
    return total


def small_dot(first, second, dims):
    return lax.dot_general(
        first, second, (dims, ((), ())), precision=lax.Precision.HIGHEST, preferred_element_type=F32
    )


def halves(value):
    high = value.astype(BF16)
    return high, (value - high.astype(F32)).astype(BF16)


def nt(first, second):
    return lax.dot_general(first, second, (((1,), (1,)), ((), ())), preferred_element_type=F32)


def gram_halves(first, second):
    (fh, fl), (sh, sl) = first, second
    return nt(fh, sh) + (nt(fh, sl) + nt(fl, sh))


def wide(ref, start, count):
    return jnp.concatenate([ref[start + k] for k in range(count)], axis=1)


def each(count, body, step=8):

    def several(start, carry):
        for k in range(step):
            body(start * step + k)
        return carry

    lax.fori_loop(0, count // step, several, 0)


def gram(first, second, unroll=False):
    step = 8

    def add(k, total):
        one = halves(wide(first, k * step, step))
        two = one if second is first else halves(wide(second, k * step, step))
        return total + gram_halves(one, two)

    start = jnp.zeros((first.shape[1], first.shape[1]), F32)
    return lax.fori_loop(0, first.shape[0] // step, add, start, unroll=unroll)


def pack(residual, own_tile, sent, first_plane, last_plane, copies, slots, plane):
    tiles = residual.shape[0]
    blocks = [residual[own_tile[s]].astype(BF16) for s in range(slots)]
    blocks.append(split_three(gram(residual, residual, unroll=True)))
    for m in range(copies):
        for s in range(slots + 1):
            sent[m * (slots + 1) + s] = blocks[s]
    for y in range(plane):
        first_plane[y] = residual[y].astype(BF16)
        last_plane[y] = residual[tiles - plane + y].astype(BF16)


def begin_kernel(copies, slots, plane, own_tile, residual, sent, first_plane, last_plane):
    pack(residual, own_tile, sent, first_plane, last_plane, copies, slots, plane)


def advance(src_count, slots, slot_tile, groups, residual, smooth, norm, image, fresh):
    tiles = residual.shape[0]
    per = slots + 1
    image[pl.ds(0, tiles)] = smooth[...]

    def add_group(i, curvature):
        for s in range(slots):
            tile = slot_tile[i * slots + s]
            image[tile] = image[tile] + groups[i * per + s].astype(F32)
        return curvature + groups[i * per + slots].astype(F32)

    start = jnp.zeros(groups.shape[1:], F32)
    curvature = join_three(lax.fori_loop(0, src_count, add_group, start))
    spread = solve_small(curvature, norm[...])

    def subtract(l):
        fresh[l] = residual[l] - mix_tile(image[l], spread)

    each(tiles, subtract)
    return spread


def step_kernel(
    src_count, copies, slots, plane, slot_tile, own_tile, groups, residual, smooth, norm,
    fresh, alpha_out, sent, first_plane, last_plane, image,
):
    alpha = advance(src_count, slots, slot_tile, groups, residual, smooth, norm, image, fresh)
    for i, row in enumerate(alpha):
        alpha_out[i] = row
    pack(fresh, own_tile, sent, first_plane, last_plane, copies, slots, plane)


def last_kernel(
    src_count, slots, slot_tile, groups, residual, smooth, norm, direction, solution,
    fresh, solution_out, image,
):
    spread = advance(src_count, slots, slot_tile, groups, residual, smooth, norm, image, fresh)

    def add(l):
        solution_out[l] = solution[l] + mix_tile(direction[l], spread)

    each(residual.shape[0], add)


def smooth_field(field, before, after, diagonal, out, plane):
    tiles = field.shape[0]
    lanes = lax.broadcasted_iota(jnp.int32, field.shape[1:], 1)
    last = field.shape[2] - 1
    end = tiles // plane - 1

    def one_plane(x, carry):
        weights = diagonal[pl.ds(pl.multiple_of(x * plane, plane), plane), :]
        for y in range(plane):
            l = x * plane + y
            tile = field[l]
            beside = jnp.where(lanes == 0, 0.0, pltpu.roll(tile, 1, 1))
            beside = beside + jnp.where(lanes == last, 0.0, pltpu.roll(tile, last, 1))
            if y > 0:
                beside = beside + field[l - 1]
            if y < plane - 1:
                beside = beside + field[l + 1]
            lower = field[jnp.maximum(l - plane, y)]
            upper = field[jnp.minimum(l + plane, end * plane + y)]
            beside = beside + jnp.where(x == 0, before[y].astype(F32), lower)
            beside = beside + jnp.where(x == end, after[y].astype(F32), upper)
            out[l] = weights[y : y + 1, :] * tile - beside
        return carry

    lax.fori_loop(0, end + 1, one_plane, 0)


def regularize_first(plane, field, before, after, diagonal, smooth, gram_own, rim_before, rim_after):
    rim_before[...] = before[...].astype(F32)
    rim_after[...] = after[...].astype(F32)
    smooth_field(field, before, after, diagonal, smooth, plane)
    gram_own[...] = gram(field, smooth)


def regularize_kernel(
    plane, field, before, after, diagonal, smooth_old, gram_own, gram_cross, fresh
):
    gram_cross[...] = gram(field, smooth_old)
    smooth_field(field, before, after, diagonal, fresh, plane)
    gram_own[...] = gram(field, fresh)


def data_kernel(first, across_x, cap, share, place, arrived, panels, row_weight, *refs):
    if first:
        gram_own, norm_out, response_out, gram_out, outgoing = refs
    else:
        (gram_own, gram_cross, gram_old, norm_old, response_old,
         norm_out, beta_out, response_out, gram_out, outgoing) = refs
    per = cap + 1
    tx_here, rows_here, width = panels.shape
    columns, block_len = arrived.shape[1:]
    foot_len = width // block_len
    total = arrived[cap].astype(F32)
    for x in range(1, across_x):
        total = total + arrived[x * per + cap].astype(F32)
    norm = join_three(total)
    norm_out[...] = norm
    beta = None
    pair = gram_own[...]
    if not first:
        rows = solve_small(norm_old[...], norm)
        for i, row in enumerate(rows):
            beta_out[i] = row
        beta = matrix_turned(rows)
        cross = small_dot(beta, gram_cross[...], ((1,), (1,)))
        inner = small_dot(beta, gram_old[...], ((1,), (0,)))
        pair = pair + cross + cross.T + small_dot(inner, beta, ((1,), (1,)))
    gram_out[...] = pair
    curvature = share * pair
    empty = jnp.zeros((columns, block_len), BF16)
    responses, weights = [], []
    for x in range(across_x):
        for s in range(cap):
            outgoing[x * per + s] = empty
    for t in range(tx_here):
        picked = jnp.concatenate([arrived[place[t, f]] for f in range(foot_len)], axis=1)
        response = nt(picked, panels[t])
        if not first:
            response = response + small_dot(beta, response_old[t], ((1,), (0,)))
        response_out[t] = response
        weighted = response * row_weight[t : t + 1, :]
        responses.append(response)
        weights.append(weighted)
    for t in range(tx_here):
        shares = jnp.dot(
            weights[t].astype(BF16), panels[t], preferred_element_type=F32
        ).astype(BF16)
        for f in range(foot_len):
            outgoing[place[t, f]] = shares[:, f * block_len : (f + 1) * block_len]
    curvature = curvature + gram_halves(
        halves(jnp.concatenate(responses, axis=1)), halves(jnp.concatenate(weights, axis=1))
    )
    pieces = split_three(curvature)
    for x in range(across_x):
        outgoing[x * per + cap] = pieces


def mix_kernel(
    plane, fresh, before, after, diagonal, direction, rim_before, rim_after, beta,
    direction_out, smooth_out, rim_before_out, rim_after_out,
):
    spread = read_rows(beta)

    def inside(l):
        direction_out[l] = fresh[l] + mix_tile(direction[l], spread)

    def beside(y):
        rim_before_out[y] = before[y].astype(F32) + mix_tile(rim_before[y], spread)
        rim_after_out[y] = after[y].astype(F32) + mix_tile(rim_after[y], spread)

    each(fresh.shape[0], inside)
    each(plane, beside, 4)
    smooth_field(direction_out, rim_before_out, rim_after_out, diagonal, smooth_out, plane)


def gather_kernel(*refs):
    count = (len(refs) - 1) // 2
    directions, alphas, out = refs[:count], refs[count : 2 * count], refs[-1]
    spreads = [read_rows(alpha) for alpha in alphas]
    for k in range(count):

        def add(l):
            term = mix_tile(directions[k][l], spreads[k])
            out[l] = term if k == 0 else out[l] + term

        each(out.shape[0], add)


def narrow_kernel(across_x, inner, slots, cap, kept, across, out):
    per = slots + 1
    total = across[slots].astype(F32)
    for y in range(1, inner):
        total = total + across[y * per + slots].astype(F32)
    pieces = split_three(join_three(total))
    for x in range(across_x):
        out[x * (cap + 1) + cap] = pieces
    for d in range(cap):
        block = across[kept[d]]
        for x in range(across_x):
            out[x * (cap + 1) + d] = block


def widen_kernel(across_x, inner, slots, cap, kept, incoming, out):
    per = slots + 1
    empty = jnp.zeros(out.shape[1:], BF16)
    for s in range(inner * per):
        out[s] = empty

    def summed(d):
        total = incoming[d].astype(F32)
        for x in range(1, across_x):
            total = total + incoming[x * (cap + 1) + d].astype(F32)
        return total

    for d in range(cap):
        out[kept[d]] = summed(d).astype(BF16)
    pieces = split_three(join_three(summed(cap)))
    for y in range(inner):
        out[y * per + slots] = pieces


def sum_kernel(copies, slots, incoming, handed):
    per = slots + 1
    for s in range(per):
        total = incoming[s].astype(F32)
        for m in range(1, copies):
            total = total + incoming[m * per + s].astype(F32)
        handed[s] = total.astype(BF16) if s < slots else split_three(join_three(total))


def owners_ranks(tile_ids, blocks_dev):
    owners = tile_ids // blocks_dev
    position = jnp.arange(tile_ids.shape[1])
    before = (owners[:, :, None] == owners[:, None, :]) & (
        position[None, None, :] < position[None, :, None]
    )
    ranking = jnp.sum(before.astype(jnp.int32), axis=2)
    return (owners, tile_ids - owners * blocks_dev, ranking)


def shards(right_side, depth_weight, panels, data_weight, footprints, counts):
    columns, extent_x, extent_y, block_len = right_side.shape
    tx_here, rows_here, foot_len, _ = panels.shape
    copies = lax.axis_size("mod")
    src_count = lax.axis_size("src")
    tiles = extent_x * extent_y
    plane = extent_y
    slots = tx_here * CAP
    per = slots + 1
    mod_index = lax.axis_index("mod")
    src_index = lax.axis_index("src")
    group_counts = lax.dynamic_slice_in_dim(counts, src_index * tx_here, tx_here, 0)
    owners_all, within_all, ranking_all = owners_ranks(footprints, tiles)
    mine = lambda ids: lax.dynamic_slice_in_dim(ids, src_index * tx_here, tx_here, 0)
    chosen = (owners_all == mod_index)[:, None, :] & (
        ranking_all[:, None, :] == jnp.arange(CAP)[None, :, None]
    )
    slot_tile = jnp.min(jnp.where(chosen, within_all[:, None, :], tiles), axis=2)
    own_tile = jnp.minimum(mine(slot_tile).reshape(-1), tiles - 1)
    slot_tile = slot_tile.reshape(-1)
    row_ids = mod_index * rows_here + jnp.arange(rows_here)
    row_weight = data_weight * (row_ids[None, :] < group_counts[:, None]).astype(F32)
    up = [(i, i + 1) for i in range(copies - 1)]
    down = [(i + 1, i) for i in range(copies - 1)]
    flat_panels = panels.reshape(tx_here, rows_here, foot_len * block_len)
    diagonal = 6.0 + depth_weight.reshape(tiles, block_len)
    share = 1.0 / src_count
    inner = INNER
    across_x = copies // inner
    along_y = [[x * inner + y for y in range(inner)] for x in range(across_x)]
    along_x = [[x * inner + y for x in range(across_x)] for y in range(inner)]

    field = ((tiles, columns, block_len), F32)
    small = ((columns, columns), F32)
    edge = ((plane, columns, block_len), BF16)
    factors = ((columns, columns, 128), F32)
    rim = ((plane, columns, block_len), F32)
    part = ((inner * per, columns, block_len), BF16)

    responses = ((tx_here, columns, rows_here), F32)
    image = pltpu.VMEM((tiles + 1, columns, block_len), F32)
    own_slots = mine(owners_all) * slots + jnp.arange(tx_here)[:, None] * CAP + mine(ranking_all)
    used = jnp.any(
        own_slots.reshape(-1)[:, None] == jnp.arange(copies * slots)[None, :], axis=0
    ).reshape(across_x, inner * slots)
    rank_used = jnp.cumsum(used.astype(jnp.int32), axis=1) - 1
    x_of = owners_all // inner
    filled = jnp.sum(
        (x_of.reshape(src_count, -1)[:, :, None] == jnp.arange(across_x)[None, None, :]).astype(
            jnp.int32
        ),
        axis=1,
    )
    all_slots = inner * slots

    def places(cap):
        at = jnp.sum(
            jnp.where(
                own_slots[:, :, None] == jnp.arange(copies * slots)[None, None, :],
                rank_used.reshape(-1)[None, None, :],
                0,
            ),
            axis=2,
        )
        place = (mine(owners_all) // inner) * (cap + 1) + at
        here = mod_index // inner
        used_here = lax.dynamic_index_in_dim(used, here, 0, keepdims=False)
        rank_here = lax.dynamic_index_in_dim(rank_used, here, 0, keepdims=False)
        slot = jnp.arange(all_slots)
        slot = (slot // slots) * per + slot % slots
        match = used_here[None, :] & (rank_here[None, :] == jnp.arange(cap)[:, None])
        kept = jnp.sum(jnp.where(match, slot[None, :], 0), axis=1)
        kept = jnp.where(jnp.any(match, axis=1), kept, slots)
        return place, kept

    residual = right_side.transpose(1, 2, 0, 3).reshape(field[0])
    sent, first_plane, last_plane = call(
        functools.partial(begin_kernel, inner, slots, plane),
        [part, edge, edge],
        (own_tile, residual),
        (SMEM, VMEM),
    )
    def along(sent, first_plane, last_plane):
        across = lax.all_to_all(sent, "mod", 0, 0, tiled=True, axis_index_groups=along_y)
        before = lax.ppermute(last_plane, "mod", up)
        after = lax.ppermute(first_plane, "mod", down)
        return across, before, after

    def iterations(cap, residual, across, before, after):
        packet = ((across_x * (cap + 1), columns, block_len), BF16)
        place, kept = places(cap)

        def reduced(outgoing):
            halfway = lax.all_to_all(
                outgoing, "mod", 0, 0, tiled=True, axis_index_groups=along_x
            )
            (halfway,) = call(
                functools.partial(widen_kernel, across_x, inner, slots, cap),
                [part],
                (kept, halfway),
                (SMEM, VMEM),
            )
            return lax.all_to_all(halfway, "mod", 0, 0, tiled=True, axis_index_groups=along_y)

        direction = smooth = norm = response = gram_pair = rim_before = rim_after = None
        directions, alphas = [], []
        for iteration in range(ITERS):
            if iteration > 0:
                across, before, after = along(sent, first_plane, last_plane)
            (narrow,) = call(
                functools.partial(narrow_kernel, across_x, inner, slots, cap),
                [packet],
                (kept, across),
                (SMEM, VMEM),
            )
            arrived = lax.all_to_all(
                narrow, "mod", 0, 0, tiled=True, axis_index_groups=along_x
            )
            if iteration == 0:
                smooth, gram_own, rim_before, rim_after = call(
                    functools.partial(regularize_first, plane),
                    [field, small, rim, rim],
                    (residual, before, after, diagonal),
                    (VMEM,) * 4,
                )
                direction = residual
                norm, response, gram_pair, outgoing = call(
                    functools.partial(data_kernel, True, across_x, cap, share),
                    [small, responses, small, packet],
                    (place, arrived, flat_panels, row_weight, gram_own),
                    (SMEM,) + (VMEM,) * 4,
                )
                incoming = reduced(outgoing)
            else:
                gram_own, gram_cross = call(
                    functools.partial(regularize_kernel, plane),
                    [small, small],
                    (residual, before, after, diagonal, smooth),
                    (VMEM,) * 5,
                    scratch=(pltpu.VMEM(field[0], F32),),
                )
                norm, beta, response, gram_pair, outgoing = call(
                    functools.partial(data_kernel, False, across_x, cap, share),
                    [small, factors, responses, small, packet],
                    (place, arrived, flat_panels, row_weight, gram_own, gram_cross,
                     gram_pair, norm, response),
                    (SMEM,) + (VMEM,) * 8,
                )
                incoming = reduced(outgoing)
                direction, smooth, rim_before, rim_after = call(
                    functools.partial(mix_kernel, plane),
                    [field, field, rim, rim],
                    (residual, before, after, diagonal,
                     direction, rim_before,
                     rim_after, beta),
                    (VMEM,) * 8,
                )
            directions.append(direction)
            if iteration + 1 == ITERS:
                (solution,) = call(
                    gather_kernel,
                    [field],
                    (*directions[:-1],
                     *alphas),
                    (VMEM,) * (2 * len(alphas)),
                )
            (handed,) = call(
                functools.partial(sum_kernel, inner, slots),
                [((per, columns, block_len), BF16)],
                (incoming,),
                (VMEM,),
            )
            groups = lax.all_gather(handed, "src", axis=0, tiled=True)
            if iteration + 1 < ITERS:
                residual, alpha, sent, first_plane, last_plane = call(
                    functools.partial(step_kernel, src_count, inner, slots, plane),
                    [field, factors, part, edge, edge],
                    (slot_tile, own_tile, groups, residual, smooth, norm),
                    (SMEM, SMEM) + (VMEM,) * 4,
                    scratch=(image,),
                )
                alphas.append(alpha)
            else:
                residual, solution = call(
                    functools.partial(last_kernel, src_count, slots),
                    [field, field],
                    (slot_tile, groups, residual, smooth, norm, direction,
                     solution),
                    (SMEM,) + (VMEM,) * 6,
                    scratch=(image,),
                )
        return solution, residual

    across, before, after = along(sent, first_plane, last_plane)
    solution, residual = lax.cond(
        jnp.all(filled <= NARROW),
        functools.partial(iterations, NARROW),
        functools.partial(iterations, all_slots),
        residual,
        across,
        before,
        after,
    )

    def to_field(parts):
        return parts.reshape(extent_x, extent_y, columns, block_len).transpose(2, 0, 1, 3)

    return (to_field(solution), to_field(residual))


def solution(mesh):
    placed = (
        P(None, "mod", None, None),
        P("mod", None, None),
        P("src", "mod", None, None),
        P("src", "mod"),
        P(),
        P(),
    )
    return jax.shard_map(
        shards,
        mesh=mesh,
        in_specs=placed,
        out_specs=(P(None, "mod", None, None), P(None, "mod", None, None)),
        check_vma=False,
    )
```

profile of v0, /device:TPU:1, one launch (start us, length us, event | category | flops | bytes accessed | tf_op | source)
XLA Modules:
  0.0 293.6 jit_solution(15630766834413573640)
XLA Ops:
  0.7 0.7 multiply_subtract_fusion
  1.4 0.7 broadcast_compare_fusion
  2.1 0.2 convert_reduce_fusion
  2.7 1.4 copy.35
  4.1 1.8 shard_map.77
  5.8 7.6 %all-to-all-start.22 = ((bf16[72,16,128]{2,1,0:T(8,128)(2,1)}), bf16[72,16,128]{2,1,0:T(8,128)(2,1)S(1)}, u32[]{:S(2)}, u32[]{:S(2)}) async-start(bf16[72,16,128]{2,1,0:T(8,128)(2,1)} %get-tuple-element.173), calls=%async_computation.22 | async-start | bytes 589824 | tf_op jit(solution)/shard_map/all_to_all | solution.py:450
  13.5 3.4 %collective-permute-start.8 = (bf16[16,16,128]{2,1,0:T(8,128)(2,1)S(1)}, bf16[16,16,128]{2,1,0:T(8,128)(2,1)S(1)}, u32[]{:S(2)}, u32[]{:S(2)}) collective-permute-start(bf16[16,16,128]{2,1,0:T(8,128)(2,1)S(1)} %get-tuple-element.174), channel_id=1, source_target_pairs={{0,1},{1,2},{2,3},{3,4},{4,5},{5,6},{6,7},{7,8},{8,9},{9,10},{10,1... | collective-permute-start | bytes 196616 | tf_op jit(solution)/shard_map/ppermute | solution.py:451
  16.9 1.3 collective-permute-start.9
  18.8 0.2 reduce_window_sum.11
  19.1 0.1 reshape.113
  19.4 0.2 convert_reduce_fusion.1
  19.6 0.6 compare_reduce_fusion
  20.9 5.8 %reshape.112 = bf16[4,96,4096]{2,1,0:T(8,128)(2,1)} reshape(bf16[4,96,32,128]{3,2,1,0:T(8,128)(2,1)} %param.10) | data formatting | bytes 6291456 | tf_op jit(solution)/shard_map/reshape | solution.py:391
  26.7 265.0 %conditional.1 = (f32[64,16,128]{2,1,0:T(8,128)S(1)}, f32[64,16,128]{2,1,0:T(8,128)S(1)}) conditional(s32[]{:T(128)} %convert_element_type.14, (s32[]{:T(128)}, pred[4,64]{1,0:T(4,128)(4,1)S(1)}, s32[4,64]{1,0:T(4,128)S(1)}, s32[]{:T(128)}, s32[64,32]{0,1:T(8,128)S(1)}, /*index=5*/s32[4,32]{0,1:T(8,128)S(1)}, bf16[72,16,128]{2,1,0:T(8,128)(2,1)S(1)}, ...), branch_computations={%region_6.10_spmd, %region_10.14_spmd} | conditional | flops 129878 | bytes 30443846 | solution.py:561
  27.3 1.6 branch_1_fun.21
  28.9 6.7 %all-to-all-start.11 = ((bf16[196,16,128]{2,1,0:T(8,128)(2,1)}), bf16[196,16,128]{2,1,0:T(8,128)(2,1)S(1)}, u32[]{:S(2)}, u32[]{:S(2)}) async-start(bf16[196,16,128]{2,1,0:T(8,128)(2,1)} %branch_1_fun.21), calls=%async_computation.11 | async-start | bytes 1605632 | tf_op jit(solution)/shard_map/cond/branch_1_fun/all_to_all | solution.py:482
  35.9 2.7 branch_1_fun.22
  38.7 0.2 select_reduce_fusion.2
  38.9 7.2 %all-to-all-done.11.arrived = bf16[196,16,128]{2,1,0:T(8,128)(2,1)S(1)} async-done(((bf16[196,16,128]{2,1,0:T(8,128)(2,1)}), bf16[196,16,128]{2,1,0:T(8,128)(2,1)S(1)}, u32[]{:S(2)}, u32[]{:S(2)}) %all-to-all-start.11) | async-done | bytes 802848 | tf_op jit(solution)/shard_map/cond/branch_1_fun/all_to_all | solution.py:482
  46.1 3.3 %branch_1_fun.23 = (f32[16,16]{1,0:T(8,128)S(1)}, f32[4,16,96]{2,1,0:T(8,128)S(1)}, f32[16,16]{1,0:T(8,128)S(1)}, bf16[196,16,128]{2,1,0:T(8,128)(2,1)S(1)}) custom-call(s32[4,32]{1,0:T(4,128)S(1)} %fusion.13.place, bf16[196,16,128]{2,1,0:T(8,128)(2,1)S(1)} %all-to-all-done.11.arrived, bf16[4,96,4096]{2,1,0:T(8,128)(2,1)} %get-tuple-element.122.panels, ...), custom_call_target="tpu_custom_call" | custom-call | tf_op jit(solution)/shard_map/cond/branch_1_fun/pallas_call | solution.py:21
  49.4 11.7 %all_to_all.99.incoming = bf16[196,16,128]{2,1,0:T(8,128)(2,1)S(1)} all-to-all(bf16[196,16,128]{2,1,0:T(8,128)(2,1)S(1)} %get-tuple-element.129), channel_id=1, replica_groups={{0,8,16,24},{1,9,17,25},{2,10,18,26},{3,11,19,27},{4,12,20,28},{5,13,21..., dimensions={0} | all-to-all | bytes 1605632 | tf_op jit(solution)/shard_map/cond/branch_1_fun/all_to_all | solution.py:460
  61.2 0.7 branch_1_fun.24
  61.9 13.2 %all_to_all.100.incoming = bf16[72,16,128]{2,1,0:T(8,128)(2,1)S(1)} all-to-all(bf16[72,16,128]{2,1,0:T(8,128)(2,1)S(1)} %branch_1_fun.24), channel_id=1, replica_groups={{0,1,2,3,4,5,6,7},{8,9,10,11,12,13,14,15},{16,17,18,19,20,21,22,23},{24..., dimensions={0} | all-to-all | bytes 589824 | tf_op jit(solution)/shard_map/cond/branch_1_fun/all_to_all | solution.py:469
  75.1 0.2 branch_1_fun.25
  75.3 31.8 %all_gather.15.groups = bf16[144,16,128]{2,1,0:T(8,128)(2,1)S(1)} all-gather(bf16[9,16,128]{2,1,0:T(8,128)(2,1)S(1)} %branch_1_fun.25), channel_id=1, replica_groups=mesh['src'=16,'mod'=32] {'src'}, dimensions={0}, use_global_device_ids=true | all-gather | bytes 626688 | tf_op jit(solution)/shard_map/cond/branch_1_fun/all_gather | solution.py:539
  107.1 2.7 branch_1_fun.26
  109.8 15.1 %all_to_all.101.across = bf16[72,16,128]{2,1,0:T(8,128)(2,1)S(1)} all-to-all(bf16[72,16,128]{2,1,0:T(8,128)(2,1)S(1)} %get-tuple-element.132), channel_id=1, replica_groups={{0,1,2,3,4,5,6,7},{8,9,10,11,12,13,14,15},{16,17,18,19,20,21,22,23},{24..., dimensions={0} | all-to-all | bytes 589824 | tf_op jit(solution)/shard_map/cond/branch_1_fun/all_to_all | solution.py:450
  124.8 1.6 branch_1_fun.27
  126.5 3.5 %all-to-all-start.15 = ((bf16[196,16,128]{2,1,0:T(8,128)(2,1)}), bf16[196,16,128]{2,1,0:T(8,128)(2,1)S(1)}, u32[]{:S(2)}, u32[]{:S(2)}) async-start(bf16[196,16,128]{2,1,0:T(8,128)(2,1)} %branch_1_fun.27), calls=%async_computation.15 | async-start | bytes 1605632 | tf_op jit(solution)/shard_map/cond/branch_1_fun/all_to_all | solution.py:482
  130.0 2.2 collective-permute-start.4
  132.2 1.3 collective-permute-start.5
  133.5 4.0 %collective-permute-done.5.after = bf16[16,16,128]{2,1,0:T(8,128)(2,1)S(1)} collective-permute-done((bf16[16,16,128]{2,1,0:T(8,128)(2,1)S(1)}, bf16[16,16,128]{2,1,0:T(8,128)(2,1)S(1)}, u32[]{:S(2)}, u32[]{:S(2)}) %collective-permute-start.5) | collective-permute-done | bytes 65568 | tf_op jit(solution)/shard_map/cond/branch_1_fun/ppermute | solution.py:452
  137.5 3.1 %branch_1_fun.28 = (f32[16,16]{1,0:T(8,128)S(1)}, f32[16,16]{1,0:T(8,128)S(1)}) custom-call(f32[64,16,128]{2,1,0:T(8,128)S(1)} %get-tuple-element.133.field.fresh.residual, bf16[16,16,128]{2,1,0:T(8,128)(2,1)S(1)} %collective-permute-done.4.before, bf16[16,16,128]{2,1,0:T(8,128)(2,1)S(1)} %collective-permute-done.5.after, ...), custom_call_target="tpu_custom_call" | custom-call | tf_op jit(solution)/shard_map/cond/branch_1_fun/pallas_call | solution.py:21
  140.6 2.4 all-to-all-done.15.arrived
  143.0 4.0 %branch_1_fun.29 = (f32[16,16]{1,0:T(8,128)S(1)}, f32[16,16,128]{2,1,0:T(8,128)S(1)}, f32[4,16,96]{2,1,0:T(8,128)S(1)}, f32[16,16]{1,0:T(8,128)S(1)}, bf16[196,16,128]{2,1,0:T(8,128)(2,1)S(1)}) custom-call(s32[4,32]{1,0:T(4,128)S(1)} %fusion.13.place, bf16[196,16,128]{2,1,0:T(8,128)(2,1)S(1)} %all-to-all-done.15.arrived, ...), custom_call_target="tpu_custom_call" | custom-call | tf_op jit(solution)/shard_map/cond/branch_1_fun/pallas_call | solution.py:21
  147.0 12.7 %all_to_all.102.incoming = bf16[196,16,128]{2,1,0:T(8,128)(2,1)S(1)} all-to-all(bf16[196,16,128]{2,1,0:T(8,128)(2,1)S(1)} %get-tuple-element.140), channel_id=1, replica_groups={{0,8,16,24},{1,9,17,25},{2,10,18,26},{3,11,19,27},{4,12,20,28},{5,13,21..., dimensions={0} | all-to-all | bytes 1605632 | tf_op jit(solution)/shard_map/cond/branch_1_fun/all_to_all | solution.py:460
  159.7 1.4 branch_1_fun.30
  161.2 4.3 %all-to-all-start.17 = ((bf16[72,16,128]{2,1,0:T(8,128)(2,1)}), bf16[72,16,128]{2,1,0:T(8,128)(2,1)S(1)}, u32[]{:S(2)}, u32[]{:S(2)}) async-start(bf16[72,16,128]{2,1,0:T(8,128)(2,1)} %branch_1_fun.30), calls=%async_computation.17 | async-start | bytes 589824 | tf_op jit(solution)/shard_map/cond/branch_1_fun/all_to_all | solution.py:469
  165.5 2.6 branch_1_fun.32
  168.1 7.1 %all-to-all-done.17.incoming = bf16[72,16,128]{2,1,0:T(8,128)(2,1)S(1)} async-done(((bf16[72,16,128]{2,1,0:T(8,128)(2,1)}), bf16[72,16,128]{2,1,0:T(8,128)(2,1)S(1)}, u32[]{:S(2)}, u32[]{:S(2)}) %all-to-all-start.17) | async-done | bytes 294944 | tf_op jit(solution)/shard_map/cond/branch_1_fun/all_to_all | solution.py:469
  175.2 0.2 branch_1_fun.31
  175.3 21.2 %all_gather.16.groups = bf16[144,16,128]{2,1,0:T(8,128)(2,1)S(1)} all-gather(bf16[9,16,128]{2,1,0:T(8,128)(2,1)S(1)} %branch_1_fun.31), channel_id=1, replica_groups=mesh['src'=16,'mod'=32] {'src'}, dimensions={0}, use_global_device_ids=true | all-gather | bytes 626688 | tf_op jit(solution)/shard_map/cond/branch_1_fun/all_gather | solution.py:539
  196.5 2.7 branch_1_fun.33
  199.3 15.1 %all_to_all.103.across = bf16[72,16,128]{2,1,0:T(8,128)(2,1)S(1)} all-to-all(bf16[72,16,128]{2,1,0:T(8,128)(2,1)S(1)} %get-tuple-element.146), channel_id=1, replica_groups={{0,1,2,3,4,5,6,7},{8,9,10,11,12,13,14,15},{16,17,18,19,20,21,22,23},{24..., dimensions={0} | all-to-all | bytes 589824 | tf_op jit(solution)/shard_map/cond/branch_1_fun/all_to_all | solution.py:450
  214.3 1.6 branch_1_fun.34
  215.9 3.6 %all-to-all-start.19 = ((bf16[196,16,128]{2,1,0:T(8,128)(2,1)}), bf16[196,16,128]{2,1,0:T(8,128)(2,1)S(1)}, u32[]{:S(2)}, u32[]{:S(2)}) async-start(bf16[196,16,128]{2,1,0:T(8,128)(2,1)} %branch_1_fun.34), calls=%async_computation.19 | async-start | bytes 1605632 | tf_op jit(solution)/shard_map/cond/branch_1_fun/all_to_all | solution.py:482
  219.6 2.2 collective-permute-start.6
  221.8 1.3 collective-permute-start.7
  223.1 4.0 %collective-permute-done.7.after = bf16[16,16,128]{2,1,0:T(8,128)(2,1)S(1)} collective-permute-done((bf16[16,16,128]{2,1,0:T(8,128)(2,1)S(1)}, bf16[16,16,128]{2,1,0:T(8,128)(2,1)S(1)}, u32[]{:S(2)}, u32[]{:S(2)}) %collective-permute-start.7) | collective-permute-done | bytes 65568 | tf_op jit(solution)/shard_map/cond/branch_1_fun/ppermute | solution.py:452
  227.1 3.1 %branch_1_fun.35 = (f32[16,16]{1,0:T(8,128)S(1)}, f32[16,16]{1,0:T(8,128)S(1)}) custom-call(f32[64,16,128]{2,1,0:T(8,128)S(1)} %get-tuple-element.147.field.fresh.residual, bf16[16,16,128]{2,1,0:T(8,128)(2,1)S(1)} %collective-permute-done.6.before, bf16[16,16,128]{2,1,0:T(8,128)(2,1)S(1)} %collective-permute-done.7.after, f32[64,128]{1,0:T(8,128)S(1)} %copy-done.27, ...), custom_call_target="tpu_custom_call" | custom-call | tf_op jit(solution)/shard_map/cond/branch_1_fun/pallas_call | solution.py:21
  230.2 2.4 all-to-all-done.19.arrived
  232.6 4.5 %branch_1_fun.36 = (f32[16,16]{1,0:T(8,128)S(1)}, f32[16,16,128]{2,1,0:T(8,128)S(1)}, f32[4,16,96]{2,1,0:T(8,128)}, f32[16,16]{1,0:T(8,128)}, bf16[196,16,128]{2,1,0:T(8,128)(2,1)S(1)}) custom-call(s32[4,32]{1,0:T(4,128)S(1)} %fusion.13.place, bf16[196,16,128]{2,1,0:T(8,128)(2,1)S(1)} %all-to-all-done.19.arrived, ...), custom_call_target="tpu_custom_call" | custom-call | tf_op jit(solution)/shard_map/cond/branch_1_fun/pallas_call | solution.py:21
  237.1 0.6 copy-done.4
  237.8 12.7 %all_to_all.104.incoming = bf16[196,16,128]{2,1,0:T(8,128)(2,1)S(1)} all-to-all(bf16[196,16,128]{2,1,0:T(8,128)(2,1)S(1)} %get-tuple-element.154), channel_id=1, replica_groups={{0,8,16,24},{1,9,17,25},{2,10,18,26},{3,11,19,27},{4,12,20,28},{5,13,21..., dimensions={0} | all-to-all | bytes 1605632 | tf_op jit(solution)/shard_map/cond/branch_1_fun/all_to_all | solution.py:460
  250.5 1.4 branch_1_fun.37
  251.9 4.3 %all-to-all-start.21 = ((bf16[72,16,128]{2,1,0:T(8,128)(2,1)}), bf16[72,16,128]{2,1,0:T(8,128)(2,1)S(1)}, u32[]{:S(2)}, u32[]{:S(2)}) async-start(bf16[72,16,128]{2,1,0:T(8,128)(2,1)} %branch_1_fun.37), calls=%async_computation.21 | async-start | bytes 589824 | tf_op jit(solution)/shard_map/cond/branch_1_fun/all_to_all | solution.py:469
  256.2 2.3 branch_1_fun.40.solution
  258.6 2.2 branch_1_fun.39
  260.8 5.1 %all-to-all-done.21.incoming = bf16[72,16,128]{2,1,0:T(8,128)(2,1)S(1)} async-done(((bf16[72,16,128]{2,1,0:T(8,128)(2,1)}), bf16[72,16,128]{2,1,0:T(8,128)(2,1)S(1)}, u32[]{:S(2)}, u32[]{:S(2)}) %all-to-all-start.21) | async-done | bytes 294944 | tf_op jit(solution)/shard_map/cond/branch_1_fun/all_to_all | solution.py:469
  265.9 0.2 branch_1_fun.38
  266.1 22.8 %all_gather.17.groups = bf16[144,16,128]{2,1,0:T(8,128)(2,1)S(1)} all-gather(bf16[9,16,128]{2,1,0:T(8,128)(2,1)S(1)} %branch_1_fun.38), channel_id=1, replica_groups=mesh['src'=16,'mod'=32] {'src'}, dimensions={0}, use_global_device_ids=true | all-gather | bytes 626688 | tf_op jit(solution)/shard_map/cond/branch_1_fun/all_gather | solution.py:539
  288.9 2.8 branch_1_fun.41
  291.7 1.0 copy.41
  292.7 1.0 copy.42
  (68 shorter events, 1.8 us)
Async XLA Ops:
  2.7 15.6 %copy-start.39 = (s32[64]{0:T(128)S(1)}, s32[64]{0:T(128)}, u32[]{:S(2)}) copy-start(s32[64]{0:T(128)} %param.13) | copy-start | bytes 772
  2.7 16.8 %copy-start.38 = (f32[4,96]{1,0:T(4,128)S(1)}, f32[4,96]{1,0:T(4,128)}, u32[]{:S(2)}) copy-start(f32[4,96]{1,0:T(4,128)} %param.11) | copy-start | bytes 4612
  2.7 16.9 %copy-start.34 = (f32[4,16,128]{2,1,0:T(8,128)S(1)}, f32[4,16,128]{2,1,0:T(8,128)}, u32[]{:S(2)}) copy-start(f32[4,16,128]{2,1,0:T(8,128)} %param.9) | copy-start | bytes 98308
  5.8 20.9 %all-to-all-start.22 = ((bf16[72,16,128]{2,1,0:T(8,128)(2,1)}), bf16[72,16,128]{2,1,0:T(8,128)(2,1)S(1)}, u32[]{:S(2)}, u32[]{:S(2)}) async-start(bf16[72,16,128]{2,1,0:T(8,128)(2,1)} %get-tuple-element.173), calls=%async_computation.22 | async-start | bytes 589824 | tf_op jit(solution)/shard_map/all_to_all | solution.py:450
  13.5 13.2 %collective-permute-start.8 = (bf16[16,16,128]{2,1,0:T(8,128)(2,1)S(1)}, bf16[16,16,128]{2,1,0:T(8,128)(2,1)S(1)}, u32[]{:S(2)}, u32[]{:S(2)}) collective-permute-start(bf16[16,16,128]{2,1,0:T(8,128)(2,1)S(1)} %get-tuple-element.174), channel_id=1, source_target_pairs={{0,1},{1,2},{2,3},{3,4},{4,5},{5,6},{6,7},{7,8},{8,9},{9,10},{10,1... | collective-permute-start | bytes 196616 | tf_op jit(solution)/shard_map/ppermute | solution.py:451
  16.9 9.8 %collective-permute-start.9 = (bf16[16,16,128]{2,1,0:T(8,128)(2,1)S(1)}, bf16[16,16,128]{2,1,0:T(8,128)(2,1)S(1)}, u32[]{:S(2)}, u32[]{:S(2)}) collective-permute-start(bf16[16,16,128]{2,1,0:T(8,128)(2,1)S(1)} %get-tuple-element.175), channel_id=1, source_target_pairs={{1,0},{2,1},{3,2},{4,3},{5,4},{6,5},{7,6},{8,7},{9,8},{10,9},{11,1... | collective-permute-start | bytes 196616 | tf_op jit(solution)/shard_map/ppermute | solution.py:452
  26.9 2.0 copy-start.29
  27.0 9.0 %copy-start.28 = (bf16[16,16,128]{2,1,0:T(8,128)(2,1)}, bf16[16,16,128]{2,1,0:T(8,128)(2,1)S(1)}, u32[]{:S(2)}) copy-start(bf16[16,16,128]{2,1,0:T(8,128)(2,1)S(1)} %get-tuple-element.125.before) | copy-start | bytes 196612 | tf_op jit(solution)/shard_map/cond
  27.0 19.1 %copy-start.21 = (f32[64,16,128]{2,1,0:T(8,128)}, f32[64,16,128]{2,1,0:T(8,128)S(1)}, u32[]{:S(2)}) copy-start(f32[64,16,128]{2,1,0:T(8,128)S(1)} %get-tuple-element.124.field.residual.direction.refs_0_) | copy-start | bytes 1572868 | tf_op jit(solution)/shard_map/cond
  27.0 116.0 %copy-start.32 = (f32[4,96]{1,0:T(4,128)}, f32[4,96]{1,0:T(4,128)S(1)}, u32[]{:S(2)}) copy-start(f32[4,96]{1,0:T(4,128)S(1)} %get-tuple-element.123.row_weight) | copy-start | bytes 4612 | tf_op jit(solution)/shard_map/cond
  27.0 138.5 %copy-start.26 = (f32[64,128]{1,0:T(8,128)}, f32[64,128]{1,0:T(8,128)S(1)}, u32[]{:S(2)}) copy-start(f32[64,128]{1,0:T(8,128)S(1)} %get-tuple-element.127.diagonal) | copy-start | bytes 98308 | tf_op jit(solution)/shard_map/cond
  27.0 169.5 %copy-start.36 = (s32[128]{0:T(128)}, s32[128]{0:T(128)S(1)}, u32[]{:S(2)}) copy-start(s32[128]{0:T(128)S(1)} %get-tuple-element.113.slot_tile) | copy-start | bytes 1540 | tf_op jit(solution)/shard_map/cond
  28.9 17.1 %all-to-all-start.11 = ((bf16[196,16,128]{2,1,0:T(8,128)(2,1)}), bf16[196,16,128]{2,1,0:T(8,128)(2,1)S(1)}, u32[]{:S(2)}, u32[]{:S(2)}) async-start(bf16[196,16,128]{2,1,0:T(8,128)(2,1)} %branch_1_fun.21), calls=%async_computation.11 | async-start | bytes 1605632 | tf_op jit(solution)/shard_map/cond/branch_1_fun/all_to_all | solution.py:482
  61.2 45.9 %copy-start.22 = (f32[64,16,128]{2,1,0:T(8,128)S(1)}, f32[64,16,128]{2,1,0:T(8,128)}, u32[]{:S(2)}) copy-start(f32[64,16,128]{2,1,0:T(8,128)} %copy-done.21) | copy-start | bytes 1572868 | tf_op jit(solution)/shard_map/cond
  126.5 16.6 %all-to-all-start.15 = ((bf16[196,16,128]{2,1,0:T(8,128)(2,1)}), bf16[196,16,128]{2,1,0:T(8,128)(2,1)S(1)}, u32[]{:S(2)}, u32[]{:S(2)}) async-start(bf16[196,16,128]{2,1,0:T(8,128)(2,1)} %branch_1_fun.27), calls=%async_computation.15 | async-start | bytes 1605632 | tf_op jit(solution)/shard_map/cond/branch_1_fun/all_to_all | solution.py:482
  130.0 3.6 %collective-permute-start.4 = (bf16[16,16,128]{2,1,0:T(8,128)(2,1)S(1)}, bf16[16,16,128]{2,1,0:T(8,128)(2,1)S(1)}, u32[]{:S(2)}, u32[]{:S(2)}) collective-permute-start(bf16[16,16,128]{2,1,0:T(8,128)(2,1)S(1)} %get-tuple-element.134), channel_id=1, source_target_pairs={{0,1},{1,2},{2,3},{3,4},{4,5},{5,6},{6,7},{7,8},{8,9},{9,10},{10,1... | collective-permute-start | bytes 196616 | tf_op jit(solution)/shard_map/cond/branch_1_fun/ppermute | solution.py:451
  132.2 5.3 %collective-permute-start.5 = (bf16[16,16,128]{2,1,0:T(8,128)(2,1)S(1)}, bf16[16,16,128]{2,1,0:T(8,128)(2,1)S(1)}, u32[]{:S(2)}, u32[]{:S(2)}) collective-permute-start(bf16[16,16,128]{2,1,0:T(8,128)(2,1)S(1)} %get-tuple-element.135), channel_id=1, source_target_pairs={{1,0},{2,1},{3,2},{4,3},{5,4},{6,5},{7,6},{8,7},{9,8},{10,9},{11,1... | collective-permute-start | bytes 196616 | tf_op jit(solution)/shard_map/cond/branch_1_fun/ppermute | solution.py:452
  161.2 14.0 %all-to-all-start.17 = ((bf16[72,16,128]{2,1,0:T(8,128)(2,1)}), bf16[72,16,128]{2,1,0:T(8,128)(2,1)S(1)}, u32[]{:S(2)}, u32[]{:S(2)}) async-start(bf16[72,16,128]{2,1,0:T(8,128)(2,1)} %branch_1_fun.30), calls=%async_computation.17 | async-start | bytes 589824 | tf_op jit(solution)/shard_map/cond/branch_1_fun/all_to_all | solution.py:469
  168.0 31.2 %copy-start = (f32[16,16,128]{2,1,0:T(8,128)}, f32[16,16,128]{2,1,0:T(8,128)S(1)}, u32[]{:S(2)}) copy-start(f32[16,16,128]{2,1,0:T(8,128)S(1)} %get-tuple-element.157.rim_after) | copy-start | bytes 393220 | tf_op jit(solution)/shard_map/cond
  215.9 11.2 %copy-start.27 = (f32[64,128]{1,0:T(8,128)S(1)}, f32[64,128]{1,0:T(8,128)}, u32[]{:S(2)}) copy-start(f32[64,128]{1,0:T(8,128)} %copy-done.26) | copy-start | bytes 98308 | tf_op jit(solution)/shard_map/cond
  215.9 16.7 %copy-start.33 = (f32[4,96]{1,0:T(4,128)S(1)}, f32[4,96]{1,0:T(4,128)}, u32[]{:S(2)}) copy-start(f32[4,96]{1,0:T(4,128)} %copy-done.32) | copy-start | bytes 4612 | tf_op jit(solution)/shard_map/cond
  215.9 16.7 %all-to-all-start.19 = ((bf16[196,16,128]{2,1,0:T(8,128)(2,1)}), bf16[196,16,128]{2,1,0:T(8,128)(2,1)S(1)}, u32[]{:S(2)}, u32[]{:S(2)}) async-start(bf16[196,16,128]{2,1,0:T(8,128)(2,1)} %branch_1_fun.34), calls=%async_computation.19 | async-start | bytes 1605632 | tf_op jit(solution)/shard_map/cond/branch_1_fun/all_to_all | solution.py:482
  219.6 3.6 %collective-permute-start.6 = (bf16[16,16,128]{2,1,0:T(8,128)(2,1)S(1)}, bf16[16,16,128]{2,1,0:T(8,128)(2,1)S(1)}, u32[]{:S(2)}, u32[]{:S(2)}) collective-permute-start(bf16[16,16,128]{2,1,0:T(8,128)(2,1)S(1)} %get-tuple-element.148), channel_id=1, source_target_pairs={{0,1},{1,2},{2,3},{3,4},{4,5},{5,6},{6,7},{7,8},{8,9},{9,10},{10,1... | collective-permute-start | bytes 196616 | tf_op jit(solution)/shard_map/cond/branch_1_fun/ppermute | solution.py:451
  221.8 5.3 %collective-permute-start.7 = (bf16[16,16,128]{2,1,0:T(8,128)(2,1)S(1)}, bf16[16,16,128]{2,1,0:T(8,128)(2,1)S(1)}, u32[]{:S(2)}, u32[]{:S(2)}) collective-permute-start(bf16[16,16,128]{2,1,0:T(8,128)(2,1)S(1)} %get-tuple-element.149), channel_id=1, source_target_pairs={{1,0},{2,1},{3,2},{4,3},{5,4},{6,5},{7,6},{8,7},{9,8},{10,9},{11,1... | collective-permute-start | bytes 196616 | tf_op jit(solution)/shard_map/cond/branch_1_fun/ppermute | solution.py:452
  237.1 0.6 copy-start.4
  251.9 14.0 %all-to-all-start.21 = ((bf16[72,16,128]{2,1,0:T(8,128)(2,1)}), bf16[72,16,128]{2,1,0:T(8,128)(2,1)S(1)}, u32[]{:S(2)}, u32[]{:S(2)}) async-start(bf16[72,16,128]{2,1,0:T(8,128)(2,1)} %branch_1_fun.37), calls=%async_computation.21 | async-start | bytes 589824 | tf_op jit(solution)/shard_map/cond/branch_1_fun/all_to_all | solution.py:469
  256.2 2.4 copy-start.1
  256.2 2.4 copy-start.5
  258.6 30.3 %copy-start.37 = (s32[128]{0:T(128)S(1)}, s32[128]{0:T(128)}, u32[]{:S(2)}) copy-start(s32[128]{0:T(128)} %copy-done.36) | copy-start | bytes 1540 | tf_op jit(solution)/shard_map/cond
where the time goes:
time: 295 us; the launch traced here: 294 us
  blocking collectives  156 us (53%)
  Pallas kernels  46.7 us (16%)
  starting transfers between devices  41.8 us (14%)
  waiting for transfers between devices  32.2 us (11%)
  local copies, waits for them, and re-layouts  11 us (4%)
  other arithmetic  3.62 us (1%)
    all_gather x3, blocking collectives, iterations(): groups = lax.all_gather(handed, 'src', axis=0, tiled=True)  75.8 us
    pallas_call x22, Pallas kernels, call(): pl.pallas_call(kernel, out_shape=[jax.ShapeDtypeStruct(shape, dtype) for...  46.7 us
    all_to_all x3, blocking collectives, reduced(): lax.all_to_all(outgoing, 'mod', 0, 0, tiled=True, axis_index_groups=along_x)  37.2 us
    all_to_all x2, blocking collectives, along(): lax.all_to_all(sent, 'mod', 0, 0, tiled=True, axis_index_groups=along_y)  30.1 us
    all_to_all x3, starting transfers between devices, iterations(): lax.all_to_all(narrow, 'mod', 0, 0, tiled=True, axis_index_groups=along_x)  13.9 us
    all_to_all x1, blocking collectives, reduced(): lax.all_to_all(halfway, 'mod', 0, 0, tiled=True, axis_index_groups=along_y)  13.2 us
    all_to_all x2, waiting for transfers between devices, reduced(): lax.all_to_all(halfway, 'mod', 0, 0, tiled=True, axis_index_groups=along_y)  12.2 us
    all_to_all x3, waiting for transfers between devices, iterations(): lax.all_to_all(narrow, 'mod', 0, 0, tiled=True, axis_index_groups=along_x)  12 us
  transfers between devices with their start and end apart: 12, of which 7 were waited for; matrix products, arithmetic and copies ran while one was open for 3% of the time, Pallas kernels for 5%

commit v1 on v0

--- a/solution.py
+++ b/solution.py
@@ -9,7 +9,7 @@
 
 CAP = 2
 INNER = 8
-NARROW = 48
+NARROW = 46
 ITERS = 3
 F32 = jnp.float32
 BF16 = jnp.bfloat16
@@ -376,19 +376,24 @@
     mod_index = lax.axis_index("mod")
     src_index = lax.axis_index("src")
     group_counts = lax.dynamic_slice_in_dim(counts, src_index * tx_here, tx_here, 0)
-    owners_all, within_all, ranking_all = owners_ranks(footprints, tiles)
-    mine = lambda ids: lax.dynamic_slice_in_dim(ids, src_index * tx_here, tx_here, 0)
-    chosen = (owners_all == mod_index)[:, None, :] & (
-        ranking_all[:, None, :] == jnp.arange(CAP)[None, :, None]
-    )
-    slot_tile = jnp.min(jnp.where(chosen, within_all[:, None, :], tiles), axis=2)
-    own_tile = jnp.minimum(mine(slot_tile).reshape(-1), tiles - 1)
-    slot_tile = slot_tile.reshape(-1)
+    group = lax.dynamic_slice_in_dim(footprints, src_index * tx_here, tx_here, 0)
+    owners, _, ranking = owners_ranks(group, tiles)
+
+    def tiles_of_slots(tile_ids):
+        its_owners, within, its_ranking = owners_ranks(tile_ids, tiles)
+        chosen = (its_owners == mod_index)[:, None, :] & (
+            its_ranking[:, None, :] == jnp.arange(CAP)[None, :, None]
+        )
+        return jnp.min(jnp.where(chosen, within[:, None, :], tiles), axis=2).reshape(-1)
+
+    own_tile = jnp.minimum(tiles_of_slots(group), tiles - 1)
     row_ids = mod_index * rows_here + jnp.arange(rows_here)
     row_weight = data_weight * (row_ids[None, :] < group_counts[:, None]).astype(F32)
     up = [(i, i + 1) for i in range(copies - 1)]
     down = [(i + 1, i) for i in range(copies - 1)]
-    flat_panels = panels.reshape(tx_here, rows_here, foot_len * block_len)
+    flat_panels = lax.optimization_barrier(
+        panels.reshape(tx_here, rows_here, foot_len * block_len)
+    )
     diagonal = 6.0 + depth_weight.reshape(tiles, block_len)
     share = 1.0 / src_count
     inner = INNER
@@ -405,12 +410,12 @@
 
     responses = ((tx_here, columns, rows_here), F32)
     image = pltpu.VMEM((tiles + 1, columns, block_len), F32)
-    own_slots = mine(owners_all) * slots + jnp.arange(tx_here)[:, None] * CAP + mine(ranking_all)
+    own_slots = owners * slots + jnp.arange(tx_here)[:, None] * CAP + ranking
     used = jnp.any(
         own_slots.reshape(-1)[:, None] == jnp.arange(copies * slots)[None, :], axis=0
     ).reshape(across_x, inner * slots)
     rank_used = jnp.cumsum(used.astype(jnp.int32), axis=1) - 1
-    x_of = owners_all // inner
+    x_of = footprints // (tiles * inner)
     filled = jnp.sum(
         (x_of.reshape(src_count, -1)[:, :, None] == jnp.arange(across_x)[None, None, :]).astype(
             jnp.int32
@@ -428,7 +433,7 @@
             ),
             axis=2,
         )
-        place = (mine(owners_all) // inner) * (cap + 1) + at
+        place = (owners // inner) * (cap + 1) + at
         here = mod_index // inner
         used_here = lax.dynamic_index_in_dim(used, here, 0, keepdims=False)
         rank_here = lax.dynamic_index_in_dim(rank_used, here, 0, keepdims=False)
@@ -446,6 +451,9 @@
         (own_tile, residual),
         (SMEM, VMEM),
     )
+    def to_field(parts):
+        return parts.reshape(extent_x, extent_y, columns, block_len).transpose(2, 0, 1, 3)
+
     def along(sent, first_plane, last_plane):
         across = lax.all_to_all(sent, "mod", 0, 0, tiled=True, axis_index_groups=along_y)
         before = lax.ppermute(last_plane, "mod", up)
@@ -455,6 +463,7 @@
     def iterations(cap, residual, across, before, after):
         packet = ((across_x * (cap + 1), columns, block_len), BF16)
         place, kept = places(cap)
+        place, slot_tile = lax.optimization_barrier((place, tiles_of_slots(footprints)))
 
         def reduced(outgoing):
             halfway = lax.all_to_all(
@@ -555,7 +564,7 @@
                     (SMEM,) + (VMEM,) * 6,
                     scratch=(image,),
                 )
-        return solution, residual
+        return to_field(solution), to_field(residual)
 
     across, before, after = along(sent, first_plane, last_plane)
     solution, residual = lax.cond(
@@ -568,10 +577,7 @@
         after,
     )
 
-    def to_field(parts):
-        return parts.reshape(extent_x, extent_y, columns, block_len).transpose(2, 0, 1, 3)
-
-    return (to_field(solution), to_field(residual))
+    return solution, residual
 
 
 def solution(mesh):

time: 295 us -> 292 us (0.990)
  no operation moved by 1% of the time
where the time goes in v1:
time: 292 us; the launch traced here: 291 us
  blocking collectives  156 us (53%)
  Pallas kernels  45.6 us (16%)
  starting transfers between devices  42 us (14%)
  waiting for transfers between devices  31.1 us (11%)
  local copies, waits for them, and re-layouts  12.3 us (4%)
    all_gather x3, blocking collectives, iterations(): groups = lax.all_gather(handed, 'src', axis=0, tiled=True)  75.2 us
    pallas_call x22, Pallas kernels, call(): pl.pallas_call(kernel, out_shape=[jax.ShapeDtypeStruct(shape, dtype) for...  45.6 us
    all_to_all x3, blocking collectives, reduced(): lax.all_to_all(outgoing, 'mod', 0, 0, tiled=True, axis_index_groups=along_x)  37 us
    all_to_all x2, blocking collectives, along(): lax.all_to_all(sent, 'mod', 0, 0, tiled=True, axis_index_groups=along_y)  30.1 us
    all_to_all x3, starting transfers between devices, iterations(): lax.all_to_all(narrow, 'mod', 0, 0, tiled=True, axis_index_groups=along_x)  13.7 us
    all_to_all x1, blocking collectives, reduced(): lax.all_to_all(halfway, 'mod', 0, 0, tiled=True, axis_index_groups=along_y)  13.3 us
    all_to_all x2, waiting for transfers between devices, reduced(): lax.all_to_all(halfway, 'mod', 0, 0, tiled=True, axis_index_groups=along_y)  12.7 us
    all_to_all x3, waiting for transfers between devices, iterations(): lax.all_to_all(narrow, 'mod', 0, 0, tiled=True, axis_index_groups=along_x)  10.4 us
  transfers between devices with their start and end apart: 12, of which 7 were waited for; matrix products, arithmetic and copies ran while one was open for 3% of the time, Pallas kernels for 5%

profile of v1, /device:TPU:1, one launch (start us, length us, event | category | flops | bytes accessed | tf_op | source)
XLA Modules:
  0.0 290.9 jit_solution(17037139586256130997)
XLA Ops:
  0.7 0.8 constant_dynamic-slice_fusion
  1.6 0.2 convert_reduce_fusion.2
  2.2 1.4 copy.43
  3.5 1.8 shard_map.87
  5.3 7.6 %all-to-all-start.22 = ((bf16[72,16,128]{2,1,0:T(8,128)(2,1)}), bf16[72,16,128]{2,1,0:T(8,128)(2,1)S(1)}, u32[]{:S(2)}, u32[]{:S(2)}) async-start(bf16[72,16,128]{2,1,0:T(8,128)(2,1)} %get-tuple-element.169), calls=%async_computation.22 | async-start | bytes 589824 | tf_op jit(solution)/shard_map/all_to_all | solution.py:458
  13.0 3.4 %collective-permute-start.8 = (bf16[16,16,128]{2,1,0:T(8,128)(2,1)S(1)}, bf16[16,16,128]{2,1,0:T(8,128)(2,1)S(1)}, u32[]{:S(2)}, u32[]{:S(2)}) collective-permute-start(bf16[16,16,128]{2,1,0:T(8,128)(2,1)S(1)} %get-tuple-element.170), channel_id=1, source_target_pairs={{0,1},{1,2},{2,3},{3,4},{4,5},{5,6},{6,7},{7,8},{8,9},{9,10},{10,1... | collective-permute-start | bytes 196616 | tf_op jit(solution)/shard_map/ppermute | solution.py:459
  16.3 1.3 collective-permute-start.9
  17.8 0.1 convert_reduce_fusion.3
  18.0 0.6 compare_reduce_fusion
  19.6 0.2 reduce_window_sum.11
  19.8 5.8 %reshape.161 = bf16[4,96,4096]{2,1,0:T(8,128)(2,1)} reshape(bf16[4,96,32,128]{3,2,1,0:T(8,128)(2,1)} %param.10) | data formatting | bytes 6291456 | tf_op jit(solution)/shard_map/reshape | solution.py:395
  25.7 265.3 %conditional.1 = (f32[16,4,16,128]{3,2,1,0:T(8,128)}, f32[16,4,16,128]{3,2,1,0:T(8,128)}) conditional(s32[]{:T(128)} %convert_element_type.21, (s32[4,32]{1,0:T(4,128)S(1)}, s32[4,32]{1,0:T(4,128)S(1)}, s32[4,64]{1,0:T(4,128)S(1)}, s32[64,32]{0,1:T(8,128)S(1)}, s32[]{:T(128)}, /*index=5*/pred[4,64]{1,0:T(4,128)(4,1)S(1)}, ...), branch_computations={%region_6.12_spmd, %region_12.18_spmd} | conditional | flops 484147 | bytes 33083224 | solution.py:570
  26.3 1.6 branch_1_fun.21
  27.9 6.7 %all-to-all-start.11 = ((bf16[188,16,128]{2,1,0:T(8,128)(2,1)}), bf16[188,16,128]{2,1,0:T(8,128)(2,1)S(1)}, u32[]{:S(2)}, u32[]{:S(2)}) async-start(bf16[188,16,128]{2,1,0:T(8,128)(2,1)} %branch_1_fun.21), calls=%async_computation.11 | async-start | bytes 1540096 | tf_op jit(solution)/shard_map/cond/branch_1_fun/all_to_all | solution.py:491
  34.8 0.2 convert_reduce_fusion.1
  35.3 0.2 select_reduce_fusion.3
  35.6 2.7 branch_1_fun.22
  38.4 6.3 %all-to-all-done.11.arrived = bf16[188,16,128]{2,1,0:T(8,128)(2,1)S(1)} async-done(((bf16[188,16,128]{2,1,0:T(8,128)(2,1)}), bf16[188,16,128]{2,1,0:T(8,128)(2,1)S(1)}, u32[]{:S(2)}, u32[]{:S(2)}) %all-to-all-start.11) | async-done | bytes 770080 | tf_op jit(solution)/shard_map/cond/branch_1_fun/all_to_all | solution.py:491
  44.7 3.3 %branch_1_fun.23 = (f32[16,16]{1,0:T(8,128)S(1)}, f32[4,16,96]{2,1,0:T(8,128)S(1)}, f32[16,16]{1,0:T(8,128)S(1)}, bf16[188,16,128]{2,1,0:T(8,128)(2,1)S(1)}) custom-call(s32[4,32]{1,0:T(4,128)S(1)} %fusion.18.place, bf16[188,16,128]{2,1,0:T(8,128)(2,1)S(1)} %all-to-all-done.11.arrived, bf16[4,96,4096]{2,1,0:T(8,128)(2,1)} %get-tuple-element.120.panels, ...), custom_call_target="tpu_custom_call" | custom-call | tf_op jit(solution)/shard_map/cond/branch_1_fun/pallas_call | solution.py:21
  48.0 11.5 %all_to_all.99.incoming = bf16[188,16,128]{2,1,0:T(8,128)(2,1)S(1)} all-to-all(bf16[188,16,128]{2,1,0:T(8,128)(2,1)S(1)} %get-tuple-element.127), channel_id=1, replica_groups={{0,8,16,24},{1,9,17,25},{2,10,18,26},{3,11,19,27},{4,12,20,28},{5,13,21..., dimensions={0} | all-to-all | bytes 1540096 | tf_op jit(solution)/shard_map/cond/branch_1_fun/all_to_all | solution.py:469
  59.6 0.7 branch_1_fun.24
  60.3 13.3 %all_to_all.100.incoming = bf16[72,16,128]{2,1,0:T(8,128)(2,1)S(1)} all-to-all(bf16[72,16,128]{2,1,0:T(8,128)(2,1)S(1)} %branch_1_fun.24), channel_id=1, replica_groups={{0,1,2,3,4,5,6,7},{8,9,10,11,12,13,14,15},{16,17,18,19,20,21,22,23},{24..., dimensions={0} | all-to-all | bytes 589824 | tf_op jit(solution)/shard_map/cond/branch_1_fun/all_to_all | solution.py:478
  73.5 0.2 branch_1_fun.25
  73.7 31.6 %all_gather.15.groups = bf16[144,16,128]{2,1,0:T(8,128)(2,1)S(1)} all-gather(bf16[9,16,128]{2,1,0:T(8,128)(2,1)S(1)} %branch_1_fun.25), channel_id=1, replica_groups=mesh['src'=16,'mod'=32] {'src'}, dimensions={0}, use_global_device_ids=true | all-gather | bytes 626688 | tf_op jit(solution)/shard_map/cond/branch_1_fun/all_gather | solution.py:548
  105.3 2.7 branch_1_fun.26
  108.0 15.1 %all_to_all.101.across = bf16[72,16,128]{2,1,0:T(8,128)(2,1)S(1)} all-to-all(bf16[72,16,128]{2,1,0:T(8,128)(2,1)S(1)} %get-tuple-element.130), channel_id=1, replica_groups={{0,1,2,3,4,5,6,7},{8,9,10,11,12,13,14,15},{16,17,18,19,20,21,22,23},{24..., dimensions={0} | all-to-all | bytes 589824 | tf_op jit(solution)/shard_map/cond/branch_1_fun/all_to_all | solution.py:458
  123.1 1.6 branch_1_fun.27
  124.7 3.5 %all-to-all-start.15 = ((bf16[188,16,128]{2,1,0:T(8,128)(2,1)}), bf16[188,16,128]{2,1,0:T(8,128)(2,1)S(1)}, u32[]{:S(2)}, u32[]{:S(2)}) async-start(bf16[188,16,128]{2,1,0:T(8,128)(2,1)} %branch_1_fun.27), calls=%async_computation.15 | async-start | bytes 1540096 | tf_op jit(solution)/shard_map/cond/branch_1_fun/all_to_all | solution.py:491
  128.2 2.2 collective-permute-start.4
  130.4 1.3 collective-permute-start.5
  131.8 4.0 %collective-permute-done.5.after = bf16[16,16,128]{2,1,0:T(8,128)(2,1)S(1)} collective-permute-done((bf16[16,16,128]{2,1,0:T(8,128)(2,1)S(1)}, bf16[16,16,128]{2,1,0:T(8,128)(2,1)S(1)}, u32[]{:S(2)}, u32[]{:S(2)}) %collective-permute-start.5) | collective-permute-done | bytes 65568 | tf_op jit(solution)/shard_map/cond/branch_1_fun/ppermute | solution.py:460
  135.7 3.1 %branch_1_fun.28 = (f32[16,16]{1,0:T(8,128)S(1)}, f32[16,16]{1,0:T(8,128)S(1)}) custom-call(f32[64,16,128]{2,1,0:T(8,128)S(1)} %get-tuple-element.131.field.fresh.residual, bf16[16,16,128]{2,1,0:T(8,128)(2,1)S(1)} %collective-permute-done.4.before, bf16[16,16,128]{2,1,0:T(8,128)(2,1)S(1)} %collective-permute-done.5.after, f32[64,128]{1,0:T(8,128)S(1)} %bitcast.32, ...), custom_call_target="tpu_custom_call" | custom-call | tf_op jit(solution)/shard_map/cond/branch_1_fun/pallas_call | solution.py:21
  138.8 2.1 all-to-all-done.15.arrived
  140.9 4.0 %branch_1_fun.29 = (f32[16,16]{1,0:T(8,128)S(1)}, f32[16,16,128]{2,1,0:T(8,128)S(1)}, f32[4,16,96]{2,1,0:T(8,128)S(1)}, f32[16,16]{1,0:T(8,128)S(1)}, bf16[188,16,128]{2,1,0:T(8,128)(2,1)S(1)}) custom-call(s32[4,32]{1,0:T(4,128)S(1)} %fusion.18.place, bf16[188,16,128]{2,1,0:T(8,128)(2,1)S(1)} %all-to-all-done.15.arrived, ...), custom_call_target="tpu_custom_call" | custom-call | tf_op jit(solution)/shard_map/cond/branch_1_fun/pallas_call | solution.py:21
  144.9 12.7 %all_to_all.102.incoming = bf16[188,16,128]{2,1,0:T(8,128)(2,1)S(1)} all-to-all(bf16[188,16,128]{2,1,0:T(8,128)(2,1)S(1)} %get-tuple-element.138), channel_id=1, replica_groups={{0,8,16,24},{1,9,17,25},{2,10,18,26},{3,11,19,27},{4,12,20,28},{5,13,21..., dimensions={0} | all-to-all | bytes 1540096 | tf_op jit(solution)/shard_map/cond/branch_1_fun/all_to_all | solution.py:469
  157.6 1.4 branch_1_fun.30
  159.0 4.4 %all-to-all-start.17 = ((bf16[72,16,128]{2,1,0:T(8,128)(2,1)}), bf16[72,16,128]{2,1,0:T(8,128)(2,1)S(1)}, u32[]{:S(2)}, u32[]{:S(2)}) async-start(bf16[72,16,128]{2,1,0:T(8,128)(2,1)} %branch_1_fun.30), calls=%async_computation.17 | async-start | bytes 589824 | tf_op jit(solution)/shard_map/cond/branch_1_fun/all_to_all | solution.py:478
  163.5 1.5 branch_1_fun.32
  165.0 0.6 copy-done.4
  165.7 7.6 %all-to-all-done.17.incoming = bf16[72,16,128]{2,1,0:T(8,128)(2,1)S(1)} async-done(((bf16[72,16,128]{2,1,0:T(8,128)(2,1)}), bf16[72,16,128]{2,1,0:T(8,128)(2,1)S(1)}, u32[]{:S(2)}, u32[]{:S(2)}) %all-to-all-start.17) | async-done | bytes 294944 | tf_op jit(solution)/shard_map/cond/branch_1_fun/all_to_all | solution.py:478
  173.3 0.2 branch_1_fun.31
  173.4 21.0 %all_gather.16.groups = bf16[144,16,128]{2,1,0:T(8,128)(2,1)S(1)} all-gather(bf16[9,16,128]{2,1,0:T(8,128)(2,1)S(1)} %branch_1_fun.31), channel_id=1, replica_groups=mesh['src'=16,'mod'=32] {'src'}, dimensions={0}, use_global_device_ids=true | all-gather | bytes 626688 | tf_op jit(solution)/shard_map/cond/branch_1_fun/all_gather | solution.py:548
  194.4 2.7 branch_1_fun.33
  197.1 15.1 %all_to_all.103.across = bf16[72,16,128]{2,1,0:T(8,128)(2,1)S(1)} all-to-all(bf16[72,16,128]{2,1,0:T(8,128)(2,1)S(1)} %get-tuple-element.144), channel_id=1, replica_groups={{0,1,2,3,4,5,6,7},{8,9,10,11,12,13,14,15},{16,17,18,19,20,21,22,23},{24..., dimensions={0} | all-to-all | bytes 589824 | tf_op jit(solution)/shard_map/cond/branch_1_fun/all_to_all | solution.py:458
  212.2 1.6 branch_1_fun.34
  213.8 3.5 %all-to-all-start.19 = ((bf16[188,16,128]{2,1,0:T(8,128)(2,1)}), bf16[188,16,128]{2,1,0:T(8,128)(2,1)S(1)}, u32[]{:S(2)}, u32[]{:S(2)}) async-start(bf16[188,16,128]{2,1,0:T(8,128)(2,1)} %branch_1_fun.34), calls=%async_computation.19 | async-start | bytes 1540096 | tf_op jit(solution)/shard_map/cond/branch_1_fun/all_to_all | solution.py:491
  217.3 2.2 collective-permute-start.6
  219.5 1.3 collective-permute-start.7
  220.8 4.0 %collective-permute-done.7.after = bf16[16,16,128]{2,1,0:T(8,128)(2,1)S(1)} collective-permute-done((bf16[16,16,128]{2,1,0:T(8,128)(2,1)S(1)}, bf16[16,16,128]{2,1,0:T(8,128)(2,1)S(1)}, u32[]{:S(2)}, u32[]{:S(2)}) %collective-permute-start.7) | collective-permute-done | bytes 65568 | tf_op jit(solution)/shard_map/cond/branch_1_fun/ppermute | solution.py:460
  224.8 3.1 %branch_1_fun.35 = (f32[16,16]{1,0:T(8,128)S(1)}, f32[16,16]{1,0:T(8,128)S(1)}) custom-call(f32[64,16,128]{2,1,0:T(8,128)S(1)} %get-tuple-element.145.field.fresh.residual, bf16[16,16,128]{2,1,0:T(8,128)(2,1)S(1)} %collective-permute-done.6.before, bf16[16,16,128]{2,1,0:T(8,128)(2,1)S(1)} %collective-permute-done.7.after, f32[64,128]{1,0:T(8,128)S(1)} %bitcast.34, ...), custom_call_target="tpu_custom_call" | custom-call | tf_op jit(solution)/shard_map/cond/branch_1_fun/pallas_call | solution.py:21
  227.9 2.1 all-to-all-done.19.arrived
  230.0 4.5 %branch_1_fun.36 = (f32[16,16]{1,0:T(8,128)S(1)}, f32[16,16,128]{2,1,0:T(8,128)S(1)}, f32[4,16,96]{2,1,0:T(8,128)}, f32[16,16]{1,0:T(8,128)}, bf16[188,16,128]{2,1,0:T(8,128)(2,1)S(1)}) custom-call(s32[4,32]{1,0:T(4,128)S(1)} %fusion.18.place, bf16[188,16,128]{2,1,0:T(8,128)(2,1)S(1)} %all-to-all-done.19.arrived, ...), custom_call_target="tpu_custom_call" | custom-call | tf_op jit(solution)/shard_map/cond/branch_1_fun/pallas_call | solution.py:21
  234.5 0.6 copy-done.8
  235.1 12.7 %all_to_all.104.incoming = bf16[188,16,128]{2,1,0:T(8,128)(2,1)S(1)} all-to-all(bf16[188,16,128]{2,1,0:T(8,128)(2,1)S(1)} %get-tuple-element.152), channel_id=1, replica_groups={{0,8,16,24},{1,9,17,25},{2,10,18,26},{3,11,19,27},{4,12,20,28},{5,13,21..., dimensions={0} | all-to-all | bytes 1540096 | tf_op jit(solution)/shard_map/cond/branch_1_fun/all_to_all | solution.py:469
  247.9 1.4 branch_1_fun.37
  249.3 4.4 %all-to-all-start.21 = ((bf16[72,16,128]{2,1,0:T(8,128)(2,1)}), bf16[72,16,128]{2,1,0:T(8,128)(2,1)S(1)}, u32[]{:S(2)}, u32[]{:S(2)}) async-start(bf16[72,16,128]{2,1,0:T(8,128)(2,1)} %branch_1_fun.37), calls=%async_computation.21 | async-start | bytes 589824 | tf_op jit(solution)/shard_map/cond/branch_1_fun/all_to_all | solution.py:478
  253.7 2.4 branch_1_fun.40.solution
  256.1 2.2 branch_1_fun.39
  258.3 5.1 %all-to-all-done.21.incoming = bf16[72,16,128]{2,1,0:T(8,128)(2,1)S(1)} async-done(((bf16[72,16,128]{2,1,0:T(8,128)(2,1)}), bf16[72,16,128]{2,1,0:T(8,128)(2,1)S(1)}, u32[]{:S(2)}, u32[]{:S(2)}) %all-to-all-start.21) | async-done | bytes 294944 | tf_op jit(solution)/shard_map/cond/branch_1_fun/all_to_all | solution.py:478
  263.5 0.2 branch_1_fun.38
  263.7 22.6 %all_gather.17.groups = bf16[144,16,128]{2,1,0:T(8,128)(2,1)S(1)} all-gather(bf16[9,16,128]{2,1,0:T(8,128)(2,1)S(1)} %branch_1_fun.38), channel_id=1, replica_groups=mesh['src'=16,'mod'=32] {'src'}, dimensions={0}, use_global_device_ids=true | all-gather | bytes 626688 | tf_op jit(solution)/shard_map/cond/branch_1_fun/all_gather | solution.py:548
  286.2 2.8 branch_1_fun.41
  289.0 1.0 copy.47
  290.0 1.0 copy.49
  (75 shorter events, 1.9 us)
Async XLA Ops:
  2.2 15.5 %copy-start.17 = (s32[64,32]{0,1:T(8,128)S(1)}, s32[64,32]{0,1:T(8,128)}, u32[]{:S(2)}) copy-start(s32[64,32]{0,1:T(8,128)} %param.12) | copy-start | bytes 24580
  5.3 20.3 %all-to-all-start.22 = ((bf16[72,16,128]{2,1,0:T(8,128)(2,1)}), bf16[72,16,128]{2,1,0:T(8,128)(2,1)S(1)}, u32[]{:S(2)}, u32[]{:S(2)}) async-start(bf16[72,16,128]{2,1,0:T(8,128)(2,1)} %get-tuple-element.169), calls=%async_computation.22 | async-start | bytes 589824 | tf_op jit(solution)/shard_map/all_to_all | solution.py:458
  13.0 12.7 %collective-permute-start.8 = (bf16[16,16,128]{2,1,0:T(8,128)(2,1)S(1)}, bf16[16,16,128]{2,1,0:T(8,128)(2,1)S(1)}, u32[]{:S(2)}, u32[]{:S(2)}) collective-permute-start(bf16[16,16,128]{2,1,0:T(8,128)(2,1)S(1)} %get-tuple-element.170), channel_id=1, source_target_pairs={{0,1},{1,2},{2,3},{3,4},{4,5},{5,6},{6,7},{7,8},{8,9},{9,10},{10,1... | collective-permute-start | bytes 196616 | tf_op jit(solution)/shard_map/ppermute | solution.py:459
  16.3 9.3 %collective-permute-start.9 = (bf16[16,16,128]{2,1,0:T(8,128)(2,1)S(1)}, bf16[16,16,128]{2,1,0:T(8,128)(2,1)S(1)}, u32[]{:S(2)}, u32[]{:S(2)}) collective-permute-start(bf16[16,16,128]{2,1,0:T(8,128)(2,1)S(1)} %get-tuple-element.171), channel_id=1, source_target_pairs={{1,0},{2,1},{3,2},{4,3},{5,4},{6,5},{7,6},{8,7},{9,8},{10,9},{11,1... | collective-permute-start | bytes 196616 | tf_op jit(solution)/shard_map/ppermute | solution.py:460
  19.8 5.9 %copy-start.20 = (f32[4,16,128]{2,1,0:T(8,128)S(1)}, f32[4,16,128]{2,1,0:T(8,128)}, u32[]{:S(2)}) copy-start(f32[4,16,128]{2,1,0:T(8,128)} %param.9) | copy-start | bytes 98308
  19.8 5.9 %copy-start.25 = (f32[4,96]{1,0:T(4,128)S(1)}, f32[4,96]{1,0:T(4,128)}, u32[]{:S(2)}) copy-start(f32[4,96]{1,0:T(4,128)} %param.11) | copy-start | bytes 4612
  19.8 5.9 %copy-start.26 = (s32[64]{0:T(128)S(1)}, s32[64]{0:T(128)}, u32[]{:S(2)}) copy-start(s32[64]{0:T(128)} %param.13) | copy-start | bytes 772
  25.9 2.0 copy-start.19
  25.9 2.0 copy-start.23
  25.9 9.7 %copy-start.18 = (bf16[16,16,128]{2,1,0:T(8,128)(2,1)}, bf16[16,16,128]{2,1,0:T(8,128)(2,1)S(1)}, u32[]{:S(2)}) copy-start(bf16[16,16,128]{2,1,0:T(8,128)(2,1)S(1)} %get-tuple-element.123.before) | copy-start | bytes 196612 | tf_op jit(solution)/shard_map/cond
  26.0 18.7 %copy-start.15 = (f32[64,16,128]{2,1,0:T(8,128)}, f32[64,16,128]{2,1,0:T(8,128)S(1)}, u32[]{:S(2)}) copy-start(f32[64,16,128]{2,1,0:T(8,128)S(1)} %get-tuple-element.122.field.residual.direction.refs_0_) | copy-start | bytes 1572868 | tf_op jit(solution)/shard_map/cond
  27.9 16.8 %all-to-all-start.11 = ((bf16[188,16,128]{2,1,0:T(8,128)(2,1)}), bf16[188,16,128]{2,1,0:T(8,128)(2,1)S(1)}, u32[]{:S(2)}, u32[]{:S(2)}) async-start(bf16[188,16,128]{2,1,0:T(8,128)(2,1)} %branch_1_fun.21), calls=%async_computation.11 | async-start | bytes 1540096 | tf_op jit(solution)/shard_map/cond/branch_1_fun/all_to_all | solution.py:491
  35.3 159.1 %copy-start.10 = (s32[128]{0:T(128)}, s32[128]{0:T(128)S(1)}, u32[]{:S(2)}) copy-start(s32[128]{0:T(128)S(1)} %reshape.153.slot_tile) | copy-start | bytes 1540 | tf_op jit(solution)/shard_map/cond
  59.6 45.8 %copy-start.16 = (f32[64,16,128]{2,1,0:T(8,128)S(1)}, f32[64,16,128]{2,1,0:T(8,128)}, u32[]{:S(2)}) copy-start(f32[64,16,128]{2,1,0:T(8,128)} %copy-done.15) | copy-start | bytes 1572868 | tf_op jit(solution)/shard_map/cond
  59.6 45.8 %copy-start.24 = (s32[8]{0:T(128)S(1)}, s32[8]{0:T(128)}, u32[]{:S(2)}) copy-start(s32[8]{0:T(128)} %copy-done.23) | copy-start | bytes 100 | tf_op jit(solution)/shard_map/cond
  124.7 16.2 %all-to-all-start.15 = ((bf16[188,16,128]{2,1,0:T(8,128)(2,1)}), bf16[188,16,128]{2,1,0:T(8,128)(2,1)S(1)}, u32[]{:S(2)}, u32[]{:S(2)}) async-start(bf16[188,16,128]{2,1,0:T(8,128)(2,1)} %branch_1_fun.27), calls=%async_computation.15 | async-start | bytes 1540096 | tf_op jit(solution)/shard_map/cond/branch_1_fun/all_to_all | solution.py:491
  128.2 3.6 %collective-permute-start.4 = (bf16[16,16,128]{2,1,0:T(8,128)(2,1)S(1)}, bf16[16,16,128]{2,1,0:T(8,128)(2,1)S(1)}, u32[]{:S(2)}, u32[]{:S(2)}) collective-permute-start(bf16[16,16,128]{2,1,0:T(8,128)(2,1)S(1)} %get-tuple-element.132), channel_id=1, source_target_pairs={{0,1},{1,2},{2,3},{3,4},{4,5},{5,6},{6,7},{7,8},{8,9},{9,10},{10,1... | collective-permute-start | bytes 196616 | tf_op jit(solution)/shard_map/cond/branch_1_fun/ppermute | solution.py:459
  130.4 5.3 %collective-permute-start.5 = (bf16[16,16,128]{2,1,0:T(8,128)(2,1)S(1)}, bf16[16,16,128]{2,1,0:T(8,128)(2,1)S(1)}, u32[]{:S(2)}, u32[]{:S(2)}) collective-permute-start(bf16[16,16,128]{2,1,0:T(8,128)(2,1)S(1)} %get-tuple-element.133), channel_id=1, source_target_pairs={{1,0},{2,1},{3,2},{4,3},{5,4},{6,5},{7,6},{8,7},{9,8},{10,9},{11,1... | collective-permute-start | bytes 196616 | tf_op jit(solution)/shard_map/cond/branch_1_fun/ppermute | solution.py:460
  159.0 14.2 %all-to-all-start.17 = ((bf16[72,16,128]{2,1,0:T(8,128)(2,1)}), bf16[72,16,128]{2,1,0:T(8,128)(2,1)S(1)}, u32[]{:S(2)}, u32[]{:S(2)}) async-start(bf16[72,16,128]{2,1,0:T(8,128)(2,1)} %branch_1_fun.30), calls=%async_computation.17 | async-start | bytes 589824 | tf_op jit(solution)/shard_map/cond/branch_1_fun/all_to_all | solution.py:478
  165.0 0.7 copy-start.4
  165.7 31.4 %copy-start.2 = (f32[16,16,128]{2,1,0:T(8,128)}, f32[16,16,128]{2,1,0:T(8,128)S(1)}, u32[]{:S(2)}) copy-start(f32[16,16,128]{2,1,0:T(8,128)S(1)} %get-tuple-element.154.rim_before) | copy-start | bytes 393220 | tf_op jit(solution)/shard_map/cond
  213.8 16.2 %all-to-all-start.19 = ((bf16[188,16,128]{2,1,0:T(8,128)(2,1)}), bf16[188,16,128]{2,1,0:T(8,128)(2,1)S(1)}, u32[]{:S(2)}, u32[]{:S(2)}) async-start(bf16[188,16,128]{2,1,0:T(8,128)(2,1)} %branch_1_fun.34), calls=%async_computation.19 | async-start | bytes 1540096 | tf_op jit(solution)/shard_map/cond/branch_1_fun/all_to_all | solution.py:491
  217.3 3.6 %collective-permute-start.6 = (bf16[16,16,128]{2,1,0:T(8,128)(2,1)S(1)}, bf16[16,16,128]{2,1,0:T(8,128)(2,1)S(1)}, u32[]{:S(2)}, u32[]{:S(2)}) collective-permute-start(bf16[16,16,128]{2,1,0:T(8,128)(2,1)S(1)} %get-tuple-element.146), channel_id=1, source_target_pairs={{0,1},{1,2},{2,3},{3,4},{4,5},{5,6},{6,7},{7,8},{8,9},{9,10},{10,1... | collective-permute-start | bytes 196616 | tf_op jit(solution)/shard_map/cond/branch_1_fun/ppermute | solution.py:459
  219.5 5.3 %collective-permute-start.7 = (bf16[16,16,128]{2,1,0:T(8,128)(2,1)S(1)}, bf16[16,16,128]{2,1,0:T(8,128)(2,1)S(1)}, u32[]{:S(2)}, u32[]{:S(2)}) collective-permute-start(bf16[16,16,128]{2,1,0:T(8,128)(2,1)S(1)} %get-tuple-element.147), channel_id=1, source_target_pairs={{1,0},{2,1},{3,2},{4,3},{5,4},{6,5},{7,6},{8,7},{9,8},{10,9},{11,1... | collective-permute-start | bytes 196616 | tf_op jit(solution)/shard_map/cond/branch_1_fun/ppermute | solution.py:460
  234.5 0.6 copy-start.8
  249.3 14.2 %all-to-all-start.21 = ((bf16[72,16,128]{2,1,0:T(8,128)(2,1)}), bf16[72,16,128]{2,1,0:T(8,128)(2,1)S(1)}, u32[]{:S(2)}, u32[]{:S(2)}) async-start(bf16[72,16,128]{2,1,0:T(8,128)(2,1)} %branch_1_fun.37), calls=%async_computation.21 | async-start | bytes 589824 | tf_op jit(solution)/shard_map/cond/branch_1_fun/all_to_all | solution.py:478
  253.7 2.4 copy-start.3
  253.7 2.4 copy-start.5
  253.7 2.4 copy-start.9
  256.1 30.1 %copy-start.11 = (s32[128]{0:T(128)S(1)}, s32[128]{0:T(128)}, u32[]{:S(2)}) copy-start(s32[128]{0:T(128)} %copy-done.10) | copy-start | bytes 1540 | tf_op jit(solution)/shard_map/cond

commit v2 on v1

--- a/solution.py
+++ b/solution.py
@@ -15,6 +15,7 @@
 BF16 = jnp.bfloat16
 VMEM = pl.BlockSpec(memory_space=pltpu.VMEM)
 SMEM = pl.BlockSpec(memory_space=pltpu.SMEM)
+ANY = pl.BlockSpec(memory_space=pl.ANY)
 
 
 def call(kernel, outs, args, specs, scratch=(), limit=16 << 20):
@@ -226,7 +227,10 @@
     gram_own[...] = gram(field, fresh)
 
 
-def data_kernel(first, across_x, cap, share, place, arrived, panels, row_weight, *refs):
+def data_kernel(first, across_x, cap, share, place, arrived, stored, row_weight, *refs):
+    refs, panels, arrival = refs[:-2], refs[-2], refs[-1]
+    coming = pltpu.make_async_copy(stored, panels, arrival)
+    coming.start()
     if first:
         gram_own, norm_out, response_out, gram_out, outgoing = refs
     else:
@@ -258,6 +262,7 @@
     for x in range(across_x):
         for s in range(cap):
             outgoing[x * per + s] = empty
+    coming.wait()
     for t in range(tx_here):
         picked = jnp.concatenate([arrived[place[t, f]] for f in range(foot_len)], axis=1)
         response = nt(picked, panels[t])
@@ -410,6 +415,10 @@
 
     responses = ((tx_here, columns, rows_here), F32)
     image = pltpu.VMEM((tiles + 1, columns, block_len), F32)
+    panel_room = (
+        pltpu.VMEM((tx_here, rows_here, foot_len * block_len), BF16),
+        pltpu.SemaphoreType.DMA(()),
+    )
     own_slots = owners * slots + jnp.arange(tx_here)[:, None] * CAP + ranking
     used = jnp.any(
         own_slots.reshape(-1)[:, None] == jnp.arange(copies * slots)[None, :], axis=0
@@ -503,7 +512,8 @@
                     functools.partial(data_kernel, True, across_x, cap, share),
                     [small, responses, small, packet],
                     (place, arrived, flat_panels, row_weight, gram_own),
-                    (SMEM,) + (VMEM,) * 4,
+                    (SMEM, VMEM, ANY) + (VMEM,) * 2,
+                    scratch=panel_room,
                 )
                 incoming = reduced(outgoing)
             else:
@@ -519,7 +529,8 @@
                     [small, factors, responses, small, packet],
                     (place, arrived, flat_panels, row_weight, gram_own, gram_cross,
                      gram_pair, norm, response),
-                    (SMEM,) + (VMEM,) * 8,
+                    (SMEM, VMEM, ANY) + (VMEM,) * 6,
+                    scratch=panel_room,
                 )
                 incoming = reduced(outgoing)
                 direction, smooth, rim_before, rim_after = call(

time: 292 us -> 294 us (level)
  no operation moved by 1% of the time
where the time goes in v2:
time: 294 us; the launch traced here: 292 us
  blocking collectives  156 us (53%)
  Pallas kernels  47.1 us (16%)
  starting transfers between devices  42 us (14%)
  waiting for transfers between devices  31.1 us (11%)
  local copies, waits for them, and re-layouts  12.2 us (4%)
    all_gather x3, blocking collectives, iterations(): groups = lax.all_gather(handed, 'src', axis=0, tiled=True)  75.2 us
    pallas_call x22, Pallas kernels, call(): pl.pallas_call(kernel, out_shape=[jax.ShapeDtypeStruct(shape, dtype) for...  47.1 us
    all_to_all x3, blocking collectives, reduced(): lax.all_to_all(outgoing, 'mod', 0, 0, tiled=True, axis_index_groups=along_x)  37 us
    all_to_all x2, blocking collectives, along(): lax.all_to_all(sent, 'mod', 0, 0, tiled=True, axis_index_groups=along_y)  30.1 us
    all_to_all x3, starting transfers between devices, iterations(): lax.all_to_all(narrow, 'mod', 0, 0, tiled=True, axis_index_groups=along_x)  13.7 us
    all_to_all x1, blocking collectives, reduced(): lax.all_to_all(halfway, 'mod', 0, 0, tiled=True, axis_index_groups=along_y)  13.3 us
    all_to_all x2, waiting for transfers between devices, reduced(): lax.all_to_all(halfway, 'mod', 0, 0, tiled=True, axis_index_groups=along_y)  12.7 us
    all_to_all x3, waiting for transfers between devices, iterations(): lax.all_to_all(narrow, 'mod', 0, 0, tiled=True, axis_index_groups=along_x)  10.4 us
  transfers between devices with their start and end apart: 12, of which 7 were waited for; matrix products, arithmetic and copies ran while one was open for 3% of the time, Pallas kernels for 5%

profile of v2, /device:TPU:1, one launch (start us, length us, event | category | flops | bytes accessed | tf_op | source)
XLA Modules:
  0.0 292.4 jit_solution(7252848790355723137)
XLA Ops:
  0.7 0.8 constant_dynamic-slice_fusion
  1.6 0.2 convert_reduce_fusion.2
  2.2 1.4 copy.43
  3.5 1.8 shard_map.87
  5.3 7.6 %all-to-all-start.22 = ((bf16[72,16,128]{2,1,0:T(8,128)(2,1)}), bf16[72,16,128]{2,1,0:T(8,128)(2,1)S(1)}, u32[]{:S(2)}, u32[]{:S(2)}) async-start(bf16[72,16,128]{2,1,0:T(8,128)(2,1)} %get-tuple-element.169), calls=%async_computation.22 | async-start | bytes 589824 | tf_op jit(solution)/shard_map/all_to_all | solution.py:467
  13.0 3.4 %collective-permute-start.8 = (bf16[16,16,128]{2,1,0:T(8,128)(2,1)S(1)}, bf16[16,16,128]{2,1,0:T(8,128)(2,1)S(1)}, u32[]{:S(2)}, u32[]{:S(2)}) collective-permute-start(bf16[16,16,128]{2,1,0:T(8,128)(2,1)S(1)} %get-tuple-element.170), channel_id=1, source_target_pairs={{0,1},{1,2},{2,3},{3,4},{4,5},{5,6},{6,7},{7,8},{8,9},{9,10},{10,1... | collective-permute-start | bytes 196616 | tf_op jit(solution)/shard_map/ppermute | solution.py:468
  16.3 1.3 collective-permute-start.9
  17.8 0.1 convert_reduce_fusion.3
  18.0 0.6 compare_reduce_fusion
  19.6 0.2 reduce_window_sum.11
  19.8 5.8 %reshape.161 = bf16[4,96,4096]{2,1,0:T(8,128)(2,1)} reshape(bf16[4,96,32,128]{3,2,1,0:T(8,128)(2,1)} %param.10) | data formatting | bytes 6291456 | tf_op jit(solution)/shard_map/reshape | solution.py:400
  25.7 266.7 %conditional.1 = (f32[16,4,16,128]{3,2,1,0:T(8,128)}, f32[16,4,16,128]{3,2,1,0:T(8,128)}) conditional(s32[]{:T(128)} %convert_element_type.21, (s32[4,32]{1,0:T(4,128)S(1)}, s32[4,32]{1,0:T(4,128)S(1)}, s32[4,64]{1,0:T(4,128)S(1)}, s32[64,32]{0,1:T(8,128)S(1)}, s32[]{:T(128)}, /*index=5*/pred[4,64]{1,0:T(4,128)(4,1)S(1)}, ...), branch_computations={%region_6.12_spmd, %region_12.18_spmd} | conditional | flops 484147 | bytes 33083224 | solution.py:581
  26.3 1.6 branch_1_fun.21
  27.9 6.7 %all-to-all-start.11 = ((bf16[188,16,128]{2,1,0:T(8,128)(2,1)}), bf16[188,16,128]{2,1,0:T(8,128)(2,1)S(1)}, u32[]{:S(2)}, u32[]{:S(2)}) async-start(bf16[188,16,128]{2,1,0:T(8,128)(2,1)} %branch_1_fun.21), calls=%async_computation.11 | async-start | bytes 1540096 | tf_op jit(solution)/shard_map/cond/branch_1_fun/all_to_all | solution.py:500
  34.8 0.2 convert_reduce_fusion.1
  35.3 0.2 select_reduce_fusion.3
  35.6 2.7 branch_1_fun.22
  38.4 6.3 %all-to-all-done.11.arrived = bf16[188,16,128]{2,1,0:T(8,128)(2,1)S(1)} async-done(((bf16[188,16,128]{2,1,0:T(8,128)(2,1)}), bf16[188,16,128]{2,1,0:T(8,128)(2,1)S(1)}, u32[]{:S(2)}, u32[]{:S(2)}) %all-to-all-start.11) | async-done | bytes 770080 | tf_op jit(solution)/shard_map/cond/branch_1_fun/all_to_all | solution.py:500
  44.7 3.9 %branch_1_fun.23 = (f32[16,16]{1,0:T(8,128)S(1)}, f32[4,16,96]{2,1,0:T(8,128)S(1)}, f32[16,16]{1,0:T(8,128)S(1)}, bf16[188,16,128]{2,1,0:T(8,128)(2,1)S(1)}) custom-call(s32[4,32]{1,0:T(4,128)S(1)} %fusion.18.place, bf16[188,16,128]{2,1,0:T(8,128)(2,1)S(1)} %all-to-all-done.11.arrived, bf16[4,96,4096]{2,1,0:T(8,128)(2,1)} %get-tuple-element.120.stored, ...), custom_call_target="tpu_custom_call" | custom-call | tf_op jit(solution)/shard_map/cond/branch_1_fun/pallas_call | solution.py:22
  48.6 11.5 %all_to_all.99.incoming = bf16[188,16,128]{2,1,0:T(8,128)(2,1)S(1)} all-to-all(bf16[188,16,128]{2,1,0:T(8,128)(2,1)S(1)} %get-tuple-element.127), channel_id=1, replica_groups={{0,8,16,24},{1,9,17,25},{2,10,18,26},{3,11,19,27},{4,12,20,28},{5,13,21..., dimensions={0} | all-to-all | bytes 1540096 | tf_op jit(solution)/shard_map/cond/branch_1_fun/all_to_all | solution.py:478
  60.2 0.7 branch_1_fun.24
  60.9 13.3 %all_to_all.100.incoming = bf16[72,16,128]{2,1,0:T(8,128)(2,1)S(1)} all-to-all(bf16[72,16,128]{2,1,0:T(8,128)(2,1)S(1)} %branch_1_fun.24), channel_id=1, replica_groups={{0,1,2,3,4,5,6,7},{8,9,10,11,12,13,14,15},{16,17,18,19,20,21,22,23},{24..., dimensions={0} | all-to-all | bytes 589824 | tf_op jit(solution)/shard_map/cond/branch_1_fun/all_to_all | solution.py:487
  74.1 0.2 branch_1_fun.25
  74.3 31.6 %all_gather.15.groups = bf16[144,16,128]{2,1,0:T(8,128)(2,1)S(1)} all-gather(bf16[9,16,128]{2,1,0:T(8,128)(2,1)S(1)} %branch_1_fun.25), channel_id=1, replica_groups=mesh['src'=16,'mod'=32] {'src'}, dimensions={0}, use_global_device_ids=true | all-gather | bytes 626688 | tf_op jit(solution)/shard_map/cond/branch_1_fun/all_gather | solution.py:559
  105.9 2.7 branch_1_fun.26
  108.6 15.1 %all_to_all.101.across = bf16[72,16,128]{2,1,0:T(8,128)(2,1)S(1)} all-to-all(bf16[72,16,128]{2,1,0:T(8,128)(2,1)S(1)} %get-tuple-element.130), channel_id=1, replica_groups={{0,1,2,3,4,5,6,7},{8,9,10,11,12,13,14,15},{16,17,18,19,20,21,22,23},{24..., dimensions={0} | all-to-all | bytes 589824 | tf_op jit(solution)/shard_map/cond/branch_1_fun/all_to_all | solution.py:467
  123.7 1.6 branch_1_fun.27
  125.3 3.5 %all-to-all-start.15 = ((bf16[188,16,128]{2,1,0:T(8,128)(2,1)}), bf16[188,16,128]{2,1,0:T(8,128)(2,1)S(1)}, u32[]{:S(2)}, u32[]{:S(2)}) async-start(bf16[188,16,128]{2,1,0:T(8,128)(2,1)} %branch_1_fun.27), calls=%async_computation.15 | async-start | bytes 1540096 | tf_op jit(solution)/shard_map/cond/branch_1_fun/all_to_all | solution.py:500
  128.8 2.2 collective-permute-start.4
  131.0 1.3 collective-permute-start.5
  132.3 4.0 %collective-permute-done.5.after = bf16[16,16,128]{2,1,0:T(8,128)(2,1)S(1)} collective-permute-done((bf16[16,16,128]{2,1,0:T(8,128)(2,1)S(1)}, bf16[16,16,128]{2,1,0:T(8,128)(2,1)S(1)}, u32[]{:S(2)}, u32[]{:S(2)}) %collective-permute-start.5) | collective-permute-done | bytes 65568 | tf_op jit(solution)/shard_map/cond/branch_1_fun/ppermute | solution.py:469
  136.3 3.1 %branch_1_fun.28 = (f32[16,16]{1,0:T(8,128)S(1)}, f32[16,16]{1,0:T(8,128)S(1)}) custom-call(f32[64,16,128]{2,1,0:T(8,128)S(1)} %get-tuple-element.131.field.fresh.residual, bf16[16,16,128]{2,1,0:T(8,128)(2,1)S(1)} %collective-permute-done.4.before, bf16[16,16,128]{2,1,0:T(8,128)(2,1)S(1)} %collective-permute-done.5.after, f32[64,128]{1,0:T(8,128)S(1)} %bitcast.32, ...), custom_call_target="tpu_custom_call" | custom-call | tf_op jit(solution)/shard_map/cond/branch_1_fun/pallas_call | solution.py:22
  139.4 2.1 all-to-all-done.15.arrived
  141.5 4.4 %branch_1_fun.29 = (f32[16,16]{1,0:T(8,128)S(1)}, f32[16,16,128]{2,1,0:T(8,128)S(1)}, f32[4,16,96]{2,1,0:T(8,128)S(1)}, f32[16,16]{1,0:T(8,128)S(1)}, bf16[188,16,128]{2,1,0:T(8,128)(2,1)S(1)}) custom-call(s32[4,32]{1,0:T(4,128)S(1)} %fusion.18.place, bf16[188,16,128]{2,1,0:T(8,128)(2,1)S(1)} %all-to-all-done.15.arrived, ...), custom_call_target="tpu_custom_call" | custom-call | tf_op jit(solution)/shard_map/cond/branch_1_fun/pallas_call | solution.py:22
  145.9 12.7 %all_to_all.102.incoming = bf16[188,16,128]{2,1,0:T(8,128)(2,1)S(1)} all-to-all(bf16[188,16,128]{2,1,0:T(8,128)(2,1)S(1)} %get-tuple-element.138), channel_id=1, replica_groups={{0,8,16,24},{1,9,17,25},{2,10,18,26},{3,11,19,27},{4,12,20,28},{5,13,21..., dimensions={0} | all-to-all | bytes 1540096 | tf_op jit(solution)/shard_map/cond/branch_1_fun/all_to_all | solution.py:478
  158.7 1.4 branch_1_fun.30
  160.1 4.4 %all-to-all-start.17 = ((bf16[72,16,128]{2,1,0:T(8,128)(2,1)}), bf16[72,16,128]{2,1,0:T(8,128)(2,1)S(1)}, u32[]{:S(2)}, u32[]{:S(2)}) async-start(bf16[72,16,128]{2,1,0:T(8,128)(2,1)} %branch_1_fun.30), calls=%async_computation.17 | async-start | bytes 589824 | tf_op jit(solution)/shard_map/cond/branch_1_fun/all_to_all | solution.py:487
  164.5 1.5 branch_1_fun.32
  166.1 0.6 copy-done.4
  166.7 7.6 %all-to-all-done.17.incoming = bf16[72,16,128]{2,1,0:T(8,128)(2,1)S(1)} async-done(((bf16[72,16,128]{2,1,0:T(8,128)(2,1)}), bf16[72,16,128]{2,1,0:T(8,128)(2,1)S(1)}, u32[]{:S(2)}, u32[]{:S(2)}) %all-to-all-start.17) | async-done | bytes 294944 | tf_op jit(solution)/shard_map/cond/branch_1_fun/all_to_all | solution.py:487
  174.3 0.2 branch_1_fun.31
  174.4 21.0 %all_gather.16.groups = bf16[144,16,128]{2,1,0:T(8,128)(2,1)S(1)} all-gather(bf16[9,16,128]{2,1,0:T(8,128)(2,1)S(1)} %branch_1_fun.31), channel_id=1, replica_groups=mesh['src'=16,'mod'=32] {'src'}, dimensions={0}, use_global_device_ids=true | all-gather | bytes 626688 | tf_op jit(solution)/shard_map/cond/branch_1_fun/all_gather | solution.py:559
  195.4 2.7 branch_1_fun.33
  198.2 15.1 %all_to_all.103.across = bf16[72,16,128]{2,1,0:T(8,128)(2,1)S(1)} all-to-all(bf16[72,16,128]{2,1,0:T(8,128)(2,1)S(1)} %get-tuple-element.144), channel_id=1, replica_groups={{0,1,2,3,4,5,6,7},{8,9,10,11,12,13,14,15},{16,17,18,19,20,21,22,23},{24..., dimensions={0} | all-to-all | bytes 589824 | tf_op jit(solution)/shard_map/cond/branch_1_fun/all_to_all | solution.py:467
  213.2 1.6 branch_1_fun.34
  214.8 3.5 %all-to-all-start.19 = ((bf16[188,16,128]{2,1,0:T(8,128)(2,1)}), bf16[188,16,128]{2,1,0:T(8,128)(2,1)S(1)}, u32[]{:S(2)}, u32[]{:S(2)}) async-start(bf16[188,16,128]{2,1,0:T(8,128)(2,1)} %branch_1_fun.34), calls=%async_computation.19 | async-start | bytes 1540096 | tf_op jit(solution)/shard_map/cond/branch_1_fun/all_to_all | solution.py:500
  218.3 2.2 collective-permute-start.6
  220.6 1.3 collective-permute-start.7
  221.9 4.0 %collective-permute-done.7.after = bf16[16,16,128]{2,1,0:T(8,128)(2,1)S(1)} collective-permute-done((bf16[16,16,128]{2,1,0:T(8,128)(2,1)S(1)}, bf16[16,16,128]{2,1,0:T(8,128)(2,1)S(1)}, u32[]{:S(2)}, u32[]{:S(2)}) %collective-permute-start.7) | collective-permute-done | bytes 65568 | tf_op jit(solution)/shard_map/cond/branch_1_fun/ppermute | solution.py:469
  225.9 3.1 %branch_1_fun.35 = (f32[16,16]{1,0:T(8,128)S(1)}, f32[16,16]{1,0:T(8,128)S(1)}) custom-call(f32[64,16,128]{2,1,0:T(8,128)S(1)} %get-tuple-element.145.field.fresh.residual, bf16[16,16,128]{2,1,0:T(8,128)(2,1)S(1)} %collective-permute-done.6.before, bf16[16,16,128]{2,1,0:T(8,128)(2,1)S(1)} %collective-permute-done.7.after, f32[64,128]{1,0:T(8,128)S(1)} %bitcast.34, ...), custom_call_target="tpu_custom_call" | custom-call | tf_op jit(solution)/shard_map/cond/branch_1_fun/pallas_call | solution.py:22
  229.0 2.1 all-to-all-done.19.arrived
  231.0 4.9 %branch_1_fun.36 = (f32[16,16]{1,0:T(8,128)S(1)}, f32[16,16,128]{2,1,0:T(8,128)S(1)}, f32[4,16,96]{2,1,0:T(8,128)}, f32[16,16]{1,0:T(8,128)}, bf16[188,16,128]{2,1,0:T(8,128)(2,1)S(1)}) custom-call(s32[4,32]{1,0:T(4,128)S(1)} %fusion.18.place, bf16[188,16,128]{2,1,0:T(8,128)(2,1)S(1)} %all-to-all-done.19.arrived, ...), custom_call_target="tpu_custom_call" | custom-call | tf_op jit(solution)/shard_map/cond/branch_1_fun/pallas_call | solution.py:22
  236.0 0.6 copy-done.8
  236.6 12.7 %all_to_all.104.incoming = bf16[188,16,128]{2,1,0:T(8,128)(2,1)S(1)} all-to-all(bf16[188,16,128]{2,1,0:T(8,128)(2,1)S(1)} %get-tuple-element.152), channel_id=1, replica_groups={{0,8,16,24},{1,9,17,25},{2,10,18,26},{3,11,19,27},{4,12,20,28},{5,13,21..., dimensions={0} | all-to-all | bytes 1540096 | tf_op jit(solution)/shard_map/cond/branch_1_fun/all_to_all | solution.py:478
  249.3 1.4 branch_1_fun.37
  250.7 4.5 %all-to-all-start.21 = ((bf16[72,16,128]{2,1,0:T(8,128)(2,1)}), bf16[72,16,128]{2,1,0:T(8,128)(2,1)S(1)}, u32[]{:S(2)}, u32[]{:S(2)}) async-start(bf16[72,16,128]{2,1,0:T(8,128)(2,1)} %branch_1_fun.37), calls=%async_computation.21 | async-start | bytes 589824 | tf_op jit(solution)/shard_map/cond/branch_1_fun/all_to_all | solution.py:487
  255.2 2.4 branch_1_fun.40.solution
  257.6 2.2 branch_1_fun.39
  259.8 5.1 %all-to-all-done.21.incoming = bf16[72,16,128]{2,1,0:T(8,128)(2,1)S(1)} async-done(((bf16[72,16,128]{2,1,0:T(8,128)(2,1)}), bf16[72,16,128]{2,1,0:T(8,128)(2,1)S(1)}, u32[]{:S(2)}, u32[]{:S(2)}) %all-to-all-start.21) | async-done | bytes 294944 | tf_op jit(solution)/shard_map/cond/branch_1_fun/all_to_all | solution.py:487
  265.0 0.2 branch_1_fun.38
  265.1 22.6 %all_gather.17.groups = bf16[144,16,128]{2,1,0:T(8,128)(2,1)S(1)} all-gather(bf16[9,16,128]{2,1,0:T(8,128)(2,1)S(1)} %branch_1_fun.38), channel_id=1, replica_groups=mesh['src'=16,'mod'=32] {'src'}, dimensions={0}, use_global_device_ids=true | all-gather | bytes 626688 | tf_op jit(solution)/shard_map/cond/branch_1_fun/all_gather | solution.py:559
  287.7 2.8 branch_1_fun.41
  290.5 1.0 copy.47
  291.5 1.0 copy.49
  (75 shorter events, 1.9 us)
Async XLA Ops:
  2.2 15.5 %copy-start.17 = (s32[64,32]{0,1:T(8,128)S(1)}, s32[64,32]{0,1:T(8,128)}, u32[]{:S(2)}) copy-start(s32[64,32]{0,1:T(8,128)} %param.12) | copy-start | bytes 24580
  5.3 20.3 %all-to-all-start.22 = ((bf16[72,16,128]{2,1,0:T(8,128)(2,1)}), bf16[72,16,128]{2,1,0:T(8,128)(2,1)S(1)}, u32[]{:S(2)}, u32[]{:S(2)}) async-start(bf16[72,16,128]{2,1,0:T(8,128)(2,1)} %get-tuple-element.169), calls=%async_computation.22 | async-start | bytes 589824 | tf_op jit(solution)/shard_map/all_to_all | solution.py:467
  13.0 12.7 %collective-permute-start.8 = (bf16[16,16,128]{2,1,0:T(8,128)(2,1)S(1)}, bf16[16,16,128]{2,1,0:T(8,128)(2,1)S(1)}, u32[]{:S(2)}, u32[]{:S(2)}) collective-permute-start(bf16[16,16,128]{2,1,0:T(8,128)(2,1)S(1)} %get-tuple-element.170), channel_id=1, source_target_pairs={{0,1},{1,2},{2,3},{3,4},{4,5},{5,6},{6,7},{7,8},{8,9},{9,10},{10,1... | collective-permute-start | bytes 196616 | tf_op jit(solution)/shard_map/ppermute | solution.py:468
  16.3 9.3 %collective-permute-start.9 = (bf16[16,16,128]{2,1,0:T(8,128)(2,1)S(1)}, bf16[16,16,128]{2,1,0:T(8,128)(2,1)S(1)}, u32[]{:S(2)}, u32[]{:S(2)}) collective-permute-start(bf16[16,16,128]{2,1,0:T(8,128)(2,1)S(1)} %get-tuple-element.171), channel_id=1, source_target_pairs={{1,0},{2,1},{3,2},{4,3},{5,4},{6,5},{7,6},{8,7},{9,8},{10,9},{11,1... | collective-permute-start | bytes 196616 | tf_op jit(solution)/shard_map/ppermute | solution.py:469
  19.8 5.9 %copy-start.20 = (f32[4,16,128]{2,1,0:T(8,128)S(1)}, f32[4,16,128]{2,1,0:T(8,128)}, u32[]{:S(2)}) copy-start(f32[4,16,128]{2,1,0:T(8,128)} %param.9) | copy-start | bytes 98308
  19.8 5.9 %copy-start.25 = (f32[4,96]{1,0:T(4,128)S(1)}, f32[4,96]{1,0:T(4,128)}, u32[]{:S(2)}) copy-start(f32[4,96]{1,0:T(4,128)} %param.11) | copy-start | bytes 4612
  19.8 5.9 %copy-start.26 = (s32[64]{0:T(128)S(1)}, s32[64]{0:T(128)}, u32[]{:S(2)}) copy-start(s32[64]{0:T(128)} %param.13) | copy-start | bytes 772
  25.9 2.0 copy-start.19
  25.9 2.0 copy-start.23
  25.9 9.7 %copy-start.18 = (bf16[16,16,128]{2,1,0:T(8,128)(2,1)}, bf16[16,16,128]{2,1,0:T(8,128)(2,1)S(1)}, u32[]{:S(2)}) copy-start(bf16[16,16,128]{2,1,0:T(8,128)(2,1)S(1)} %get-tuple-element.123.before) | copy-start | bytes 196612 | tf_op jit(solution)/shard_map/cond
  26.0 18.7 %copy-start.15 = (f32[64,16,128]{2,1,0:T(8,128)}, f32[64,16,128]{2,1,0:T(8,128)S(1)}, u32[]{:S(2)}) copy-start(f32[64,16,128]{2,1,0:T(8,128)S(1)} %get-tuple-element.122.field.residual.direction.refs_0_) | copy-start | bytes 1572868 | tf_op jit(solution)/shard_map/cond
  27.9 16.8 %all-to-all-start.11 = ((bf16[188,16,128]{2,1,0:T(8,128)(2,1)}), bf16[188,16,128]{2,1,0:T(8,128)(2,1)S(1)}, u32[]{:S(2)}, u32[]{:S(2)}) async-start(bf16[188,16,128]{2,1,0:T(8,128)(2,1)} %branch_1_fun.21), calls=%async_computation.11 | async-start | bytes 1540096 | tf_op jit(solution)/shard_map/cond/branch_1_fun/all_to_all | solution.py:500
  35.3 160.2 %copy-start.10 = (s32[128]{0:T(128)}, s32[128]{0:T(128)S(1)}, u32[]{:S(2)}) copy-start(s32[128]{0:T(128)S(1)} %reshape.153.slot_tile) | copy-start | bytes 1540 | tf_op jit(solution)/shard_map/cond
  60.2 45.8 %copy-start.16 = (f32[64,16,128]{2,1,0:T(8,128)S(1)}, f32[64,16,128]{2,1,0:T(8,128)}, u32[]{:S(2)}) copy-start(f32[64,16,128]{2,1,0:T(8,128)} %copy-done.15) | copy-start | bytes 1572868 | tf_op jit(solution)/shard_map/cond
  60.2 45.8 %copy-start.24 = (s32[8]{0:T(128)S(1)}, s32[8]{0:T(128)}, u32[]{:S(2)}) copy-start(s32[8]{0:T(128)} %copy-done.23) | copy-start | bytes 100 | tf_op jit(solution)/shard_map/cond
  125.3 16.2 %all-to-all-start.15 = ((bf16[188,16,128]{2,1,0:T(8,128)(2,1)}), bf16[188,16,128]{2,1,0:T(8,128)(2,1)S(1)}, u32[]{:S(2)}, u32[]{:S(2)}) async-start(bf16[188,16,128]{2,1,0:T(8,128)(2,1)} %branch_1_fun.27), calls=%async_computation.15 | async-start | bytes 1540096 | tf_op jit(solution)/shard_map/cond/branch_1_fun/all_to_all | solution.py:500
  128.8 3.6 %collective-permute-start.4 = (bf16[16,16,128]{2,1,0:T(8,128)(2,1)S(1)}, bf16[16,16,128]{2,1,0:T(8,128)(2,1)S(1)}, u32[]{:S(2)}, u32[]{:S(2)}) collective-permute-start(bf16[16,16,128]{2,1,0:T(8,128)(2,1)S(1)} %get-tuple-element.132), channel_id=1, source_target_pairs={{0,1},{1,2},{2,3},{3,4},{4,5},{5,6},{6,7},{7,8},{8,9},{9,10},{10,1... | collective-permute-start | bytes 196616 | tf_op jit(solution)/shard_map/cond/branch_1_fun/ppermute | solution.py:468
  131.0 5.3 %collective-permute-start.5 = (bf16[16,16,128]{2,1,0:T(8,128)(2,1)S(1)}, bf16[16,16,128]{2,1,0:T(8,128)(2,1)S(1)}, u32[]{:S(2)}, u32[]{:S(2)}) collective-permute-start(bf16[16,16,128]{2,1,0:T(8,128)(2,1)S(1)} %get-tuple-element.133), channel_id=1, source_target_pairs={{1,0},{2,1},{3,2},{4,3},{5,4},{6,5},{7,6},{8,7},{9,8},{10,9},{11,1... | collective-permute-start | bytes 196616 | tf_op jit(solution)/shard_map/cond/branch_1_fun/ppermute | solution.py:469
  160.1 14.2 %all-to-all-start.17 = ((bf16[72,16,128]{2,1,0:T(8,128)(2,1)}), bf16[72,16,128]{2,1,0:T(8,128)(2,1)S(1)}, u32[]{:S(2)}, u32[]{:S(2)}) async-start(bf16[72,16,128]{2,1,0:T(8,128)(2,1)} %branch_1_fun.30), calls=%async_computation.17 | async-start | bytes 589824 | tf_op jit(solution)/shard_map/cond/branch_1_fun/all_to_all | solution.py:487
  166.0 0.7 copy-start.4
  166.7 31.5 %copy-start.2 = (f32[16,16,128]{2,1,0:T(8,128)}, f32[16,16,128]{2,1,0:T(8,128)S(1)}, u32[]{:S(2)}) copy-start(f32[16,16,128]{2,1,0:T(8,128)S(1)} %get-tuple-element.154.rim_before) | copy-start | bytes 393220 | tf_op jit(solution)/shard_map/cond
  214.8 16.2 %all-to-all-start.19 = ((bf16[188,16,128]{2,1,0:T(8,128)(2,1)}), bf16[188,16,128]{2,1,0:T(8,128)(2,1)S(1)}, u32[]{:S(2)}, u32[]{:S(2)}) async-start(bf16[188,16,128]{2,1,0:T(8,128)(2,1)} %branch_1_fun.34), calls=%async_computation.19 | async-start | bytes 1540096 | tf_op jit(solution)/shard_map/cond/branch_1_fun/all_to_all | solution.py:500
  218.3 3.6 %collective-permute-start.6 = (bf16[16,16,128]{2,1,0:T(8,128)(2,1)S(1)}, bf16[16,16,128]{2,1,0:T(8,128)(2,1)S(1)}, u32[]{:S(2)}, u32[]{:S(2)}) collective-permute-start(bf16[16,16,128]{2,1,0:T(8,128)(2,1)S(1)} %get-tuple-element.146), channel_id=1, source_target_pairs={{0,1},{1,2},{2,3},{3,4},{4,5},{5,6},{6,7},{7,8},{8,9},{9,10},{10,1... | collective-permute-start | bytes 196616 | tf_op jit(solution)/shard_map/cond/branch_1_fun/ppermute | solution.py:468
  220.6 5.3 %collective-permute-start.7 = (bf16[16,16,128]{2,1,0:T(8,128)(2,1)S(1)}, bf16[16,16,128]{2,1,0:T(8,128)(2,1)S(1)}, u32[]{:S(2)}, u32[]{:S(2)}) collective-permute-start(bf16[16,16,128]{2,1,0:T(8,128)(2,1)S(1)} %get-tuple-element.147), channel_id=1, source_target_pairs={{1,0},{2,1},{3,2},{4,3},{5,4},{6,5},{7,6},{8,7},{9,8},{10,9},{11,1... | collective-permute-start | bytes 196616 | tf_op jit(solution)/shard_map/cond/branch_1_fun/ppermute | solution.py:469
  236.0 0.6 copy-start.8
  250.7 14.2 %all-to-all-start.21 = ((bf16[72,16,128]{2,1,0:T(8,128)(2,1)}), bf16[72,16,128]{2,1,0:T(8,128)(2,1)S(1)}, u32[]{:S(2)}, u32[]{:S(2)}) async-start(bf16[72,16,128]{2,1,0:T(8,128)(2,1)} %branch_1_fun.37), calls=%async_computation.21 | async-start | bytes 589824 | tf_op jit(solution)/shard_map/cond/branch_1_fun/all_to_all | solution.py:487
  255.2 2.4 copy-start.3
  255.2 2.4 copy-start.5
  255.2 2.4 copy-start.9
  257.6 30.1 %copy-start.11 = (s32[128]{0:T(128)S(1)}, s32[128]{0:T(128)}, u32[]{:S(2)}) copy-start(s32[128]{0:T(128)} %copy-done.10) | copy-start | bytes 1540 | tf_op jit(solution)/shard_map/cond
